TPU v7x, 32 devices: a whole 2x2x4 slice. The times are simulated.
32 devices in a mesh: rep: 4 (over z), fsdp: 4 (over x, core), ctx: 2 (over y).
Axes of the slice: x: 2, y: 2, z: 4, core: 2. Of those that a mesh axis runs over, the one named last changes fastest.
Arguments:
- residual_in: bfloat16 [16, 1024, 1024], P(('rep', 'fsdp'), 'ctx'), may hold values from -6 to 6
- block_order: int32 [16, 4], P(('rep', 'fsdp')), may hold values from 0 to 3, each once within a row
- ln1_gain: bfloat16 [1024], P('fsdp'), may hold values from 0.25 to 1.75
- ln1_bias: bfloat16 [1024], P('fsdp'), may hold values from -4 to 4
- ln2_gain: bfloat16 [1024], P('fsdp'), may hold values from 0.25 to 1.75
- ln2_bias: bfloat16 [1024], P('fsdp'), may hold values from -4 to 4
- w_qkv: bfloat16 [1024, 3072], P('fsdp'), may hold values from -0.1875 to 0.1875
- b_qkv: bfloat16 [3072], P('fsdp'), may hold values from -4 to 4
- w_out: bfloat16 [1024, 1024], P('fsdp'), may hold values from -0.75 to 0.75
- b_out: bfloat16 [1024], P('fsdp'), may hold values from -4 to 4
- w_up: bfloat16 [1024, 4096], P('fsdp'), may hold values from -0.1875 to 0.1875
- b_up: bfloat16 [4096], P('fsdp'), may hold values from -6 to 6
- w_down: bfloat16 [4096, 1024], P('fsdp'), may hold values from -0.09375 to 0.09375
- b_down: bfloat16 [1024], P('fsdp'), may hold values from -4 to 4
- cotangent: bfloat16 [16, 1024, 1024], P(('rep', 'fsdp'), 'ctx'), may hold values from -6 to 6
Outputs:
- out: bfloat16 [16, 1024, 1024], P(('rep', 'fsdp'), 'ctx')
- grad_input: float32 [16, 1024, 1024], P(('rep', 'fsdp'), 'ctx')
- grad_ln1_gain: float32 [1024], P('fsdp')
- grad_ln1_bias: float32 [1024], P('fsdp')
- grad_ln2_gain: float32 [1024], P('fsdp')
- grad_ln2_bias: float32 [1024], P('fsdp')
- grad_w_qkv: float32 [1024, 3072], P('fsdp')
- grad_b_qkv: float32 [3072], P('fsdp')
- grad_w_out: float32 [1024, 1024], P('fsdp')
- grad_b_out: float32 [1024], P('fsdp')
- grad_w_up: float32 [1024, 4096], P('fsdp')
- grad_b_up: float32 [4096], P('fsdp')
- grad_w_down: float32 [4096, 1024], P('fsdp')
- grad_b_down: float32 [1024], P('fsdp')
Inputs may be any that keep to these rules, and one draw needn't show every extreme that they name: Each row is a permutation of the block numbers of one sequence; block slot b (storage slots b * 256 to (b + 1) * 256 - 1) holds the sequence's block block_order[s, b].
All inputs are finite; a program needn't handle non-finite values.
Results may differ from a plain program's by a relative error of at most 0.01.
Values may be sent and summed in bfloat16 or wider, within the bound.
A program may use at most 192 MiB of HBM per device.

v0:
```python
import math

import jax
import jax.numpy as jnp
from jax import lax
from jax.sharding import PartitionSpec as P

HEADS = 16
HEAD = 64
ROT = 16
BLK = 256


EPSILON = 1e-05


def layer_norm(values, gain_vec, bias_vec):
    center = values - jnp.mean(values, -1, keepdims=True)
    spread = jnp.mean(center * center, -1, keepdims=True)
    return center * lax.rsqrt(spread + EPSILON) * gain_vec + bias_vec


def rotary_tables(positions):
    halves = ROT // 2
    inverse = 10000.0 ** (-(2.0 * jnp.arange(halves, dtype=jnp.float32)) / ROT)
    angles = positions.astype(jnp.float32)[:, None] * inverse[None, :]
    return (jnp.cos(angles)[:, None, :], jnp.sin(angles)[:, None, :])


def turn(values, cosine, sine_tab):
    halves = ROT // 2
    first_half = values[..., :halves]
    second_half = values[..., halves:ROT]
    return jnp.concatenate(
        [
            first_half * cosine - second_half * sine_tab,
            second_half * cosine + first_half * sine_tab,
            values[..., ROT:],
        ],
        -1,
    )


def gelu_exact(values):
    return jax.nn.gelu(values, approximate=False)


def masked_scores(query_blk, key_blk, query_pos, key_pos):
    factor = 1.0 / math.sqrt(HEAD)
    scores = (
        jnp.einsum("qgd,kgd->gqk", query_blk, key_blk, preferred_element_type=jnp.float32) * factor
    )
    allowed = key_pos[None, None, :] <= query_pos[None, :, None]
    return (jnp.where(allowed, scores, -1e30), allowed)


def attend_forward(query_blk, key_blk, value_blk, query_pos, key_pos):
    scores, allowed = masked_scores(query_blk, key_blk, query_pos, key_pos)
    row_max = jnp.max(scores, -1, keepdims=True)
    expval = jnp.exp(scores - row_max)
    row_sum = jnp.sum(expval, -1, keepdims=True)
    probability = (expval / row_sum).astype(jnp.bfloat16)
    context = jnp.einsum("gqk,kgd->qgd", probability, value_blk, preferred_element_type=jnp.float32)
    return (context, (row_max + jnp.log(row_sum))[:, :, 0])


def attend_back(query_blk, key_blk, value_blk, query_pos, key_pos, log_total, grad_ctx):
    factor = 1.0 / math.sqrt(HEAD)
    scores, allowed = masked_scores(query_blk, key_blk, query_pos, key_pos)
    probability = jnp.where(allowed, jnp.exp(scores - log_total[:, :, None]), 0.0)
    grad_value = jnp.einsum(
        "gqk,qgd->kgd",
        probability.astype(jnp.bfloat16),
        grad_ctx,
        preferred_element_type=jnp.float32,
    )
    grad_prob = jnp.einsum("qgd,kgd->gqk", grad_ctx, value_blk, preferred_element_type=jnp.float32)
    grad_score = probability * (grad_prob - jnp.sum(probability * grad_prob, -1, keepdims=True))
    score_low = grad_score.astype(jnp.bfloat16)
    grad_query = (
        jnp.einsum("gqk,kgd->qgd", score_low, key_blk, preferred_element_type=jnp.float32) * factor
    )
    grad_key = (
        jnp.einsum("gqk,qgd->kgd", score_low, query_blk, preferred_element_type=jnp.float32)
        * factor
    )
    return (grad_query, grad_key, grad_value)


def body(
    residual_in,
    block_order,
    ln1_gain,
    ln1_bias,
    ln2_gain,
    ln2_bias,
    w_qkv,
    b_qkv,
    w_out,
    b_out,
    w_up,
    b_up,
    w_down,
    b_down,
    cotangent,
):
    seq_count, local_rows, model_width = residual_in.shape
    ctx_count = lax.axis_size("ctx")
    key_len = local_rows * ctx_count
    row_count = seq_count * local_rows
    step_rows = min(local_rows, 512)
    query_blocks = local_rows // step_rows
    head_group = min(HEADS, 4)
    groups = HEADS // head_group
    column_width = head_group * HEAD
    total_steps = seq_count * query_blocks * groups
    slot_ids = jnp.arange(key_len, dtype=jnp.int32)
    key_positions = block_order[:, slot_ids // BLK] * BLK + slot_ids % BLK
    query_positions = lax.dynamic_slice_in_dim(
        key_positions, lax.axis_index("ctx") * local_rows, local_rows, 1
    )
    inputs = residual_in.reshape(row_count, model_width).astype(jnp.float32)
    gain_one, bias_one, gain_two, bias_two, full_qkv, full_qkv_bias, full_up, full_up_bias = (
        lax.all_gather(ln1_gain, "fsdp", axis=0, tiled=True),
        lax.all_gather(ln1_bias, "fsdp", axis=0, tiled=True),
        lax.all_gather(ln2_gain, "fsdp", axis=0, tiled=True),
        lax.all_gather(ln2_bias, "fsdp", axis=0, tiled=True),
        lax.all_gather(w_qkv, "fsdp", axis=0, tiled=True),
        lax.all_gather(b_qkv, "fsdp", axis=0, tiled=True),
        lax.all_gather(w_up, "fsdp", axis=0, tiled=True),
        lax.all_gather(b_up, "fsdp", axis=0, tiled=True),
    )
    normed_one = layer_norm(
        inputs, gain_one.astype(jnp.float32), bias_one.astype(jnp.float32)
    ).astype(jnp.bfloat16)
    projected = jnp.dot(
        normed_one, full_qkv, preferred_element_type=jnp.float32
    ) + full_qkv_bias.astype(jnp.float32)
    cosine, sine_tab = rotary_tables(query_positions.reshape(row_count))
    queries = (
        turn(projected[:, :model_width].reshape(row_count, HEADS, HEAD), cosine, sine_tab)
        .astype(jnp.bfloat16)
        .reshape(seq_count, local_rows, model_width)
    )
    keys_own = (
        turn(
            projected[:, model_width : 2 * model_width].reshape(row_count, HEADS, HEAD),
            cosine,
            sine_tab,
        )
        .astype(jnp.bfloat16)
        .reshape(seq_count, local_rows, model_width)
    )
    values_own = (
        projected[:, 2 * model_width :]
        .astype(jnp.bfloat16)
        .reshape(seq_count, local_rows, model_width)
    )
    keys_seen, values_seen = (
        lax.all_gather(keys_own, "ctx", axis=1, tiled=True),
        lax.all_gather(values_own, "ctx", axis=1, tiled=True),
    )
    normed_two = layer_norm(
        inputs, gain_two.astype(jnp.float32), bias_two.astype(jnp.float32)
    ).astype(jnp.bfloat16)
    hidden_pre = jnp.dot(
        normed_two, full_up, preferred_element_type=jnp.float32
    ) + full_up_bias.astype(jnp.float32)
    hidden = gelu_exact(hidden_pre).astype(jnp.bfloat16)

    def locate(number):
        seq_idx = number // (query_blocks * groups)
        block_idx = number // groups % query_blocks
        head_idx = number % groups
        return (seq_idx, block_idx * step_rows, head_idx * column_width)

    def slab_of(array, seq_idx, row_start, length, column):
        return lax.dynamic_slice(
            array, (seq_idx, row_start, column), (1, length, column_width)
        ).reshape(length, head_group, HEAD)

    def step_inputs(number):
        seq_idx, row_start, column = locate(number)
        query_pos = query_positions[0]
        key_pos = key_positions[0]
        query_blk = slab_of(queries, seq_idx, row_start, step_rows, column)
        key_blk = slab_of(keys_seen, seq_idx, 0, key_len, column)
        value_blk = slab_of(values_seen, seq_idx, 0, key_len, column)
        return (query_blk, key_blk, value_blk, query_pos, key_pos)

    def forward_step(number):
        query_blk, key_blk, value_blk, query_pos, key_pos = step_inputs(number)
        return attend_forward(query_blk, key_blk, value_blk, query_pos, key_pos)

    step_ids = jnp.arange(total_steps, dtype=jnp.int32)
    mixed_heads, log_total = lax.map(forward_step, step_ids)
    context = (
        mixed_heads.reshape(seq_count, query_blocks, groups, step_rows, column_width)
        .transpose(0, 1, 3, 2, 4)
        .reshape(row_count, model_width)
        .astype(jnp.bfloat16)
    )
    full_out, full_out_bias, full_down, full_down_bias = (
        lax.all_gather(w_out, "fsdp", axis=0, tiled=True),
        lax.all_gather(b_out, "fsdp", axis=0, tiled=True),
        lax.all_gather(w_down, "fsdp", axis=0, tiled=True),
        lax.all_gather(b_down, "fsdp", axis=0, tiled=True),
    )
    attention = jnp.dot(
        context, full_out, preferred_element_type=jnp.float32
    ) + full_out_bias.astype(jnp.float32)
    feed_out = jnp.dot(
        hidden, full_down, preferred_element_type=jnp.float32
    ) + full_down_bias.astype(jnp.float32)
    result = (
        (inputs + attention + feed_out)
        .astype(jnp.bfloat16)
        .reshape(seq_count, local_rows, model_width)
    )
    upstream = cotangent.reshape(row_count, model_width)
    upstream_f = upstream.astype(jnp.float32)
    back_out, back_down = (
        lax.all_gather(w_out, "fsdp", axis=0, tiled=True),
        lax.all_gather(w_down, "fsdp", axis=0, tiled=True),
    )
    back_gain_one, back_gain_two, back_qkv, back_up = (
        lax.all_gather(ln1_gain, "fsdp", axis=0, tiled=True),
        lax.all_gather(ln2_gain, "fsdp", axis=0, tiled=True),
        lax.all_gather(w_qkv, "fsdp", axis=0, tiled=True),
        lax.all_gather(w_up, "fsdp", axis=0, tiled=True),
    )
    grad_out_bias = jnp.sum(upstream_f, 0)
    grad_down = jnp.einsum("nf,nd->fd", hidden, upstream, preferred_element_type=jnp.float32)
    grad_out = jnp.einsum("nc,nd->cd", context, upstream, preferred_element_type=jnp.float32)
    grad_context = (
        jnp.einsum("nd,cd->nc", upstream, back_out, preferred_element_type=jnp.float32)
        .astype(jnp.bfloat16)
        .reshape(seq_count, local_rows, model_width)
    )

    def backward_step(number):
        query_blk, key_blk, value_blk, query_pos, key_pos = step_inputs(number)
        seq_idx, row_start, column = locate(number)
        grad_blk = slab_of(grad_context, seq_idx, row_start, step_rows, column)
        return attend_back(
            query_blk, key_blk, value_blk, query_pos, key_pos, log_total[number], grad_blk
        )

    grad_q_steps, grad_k_steps, grad_v_steps = lax.map(backward_step, step_ids)

    def keyed(steps_arr):
        summed = jnp.sum(
            steps_arr.reshape(seq_count, query_blocks, groups, key_len, column_width), 1
        )
        return summed.transpose(0, 2, 1, 3).reshape(seq_count, key_len, model_width)

    grad_hidden = jnp.einsum("nd,fd->nf", upstream, back_down, preferred_element_type=jnp.float32)
    gelu_pull = jax.vjp(gelu_exact, hidden_pre)[1]
    grad_pre = gelu_pull(grad_hidden)[0].astype(jnp.bfloat16)
    grad_up = jnp.einsum("nd,nf->df", normed_two, grad_pre, preferred_element_type=jnp.float32)
    grad_up_bias = jnp.sum(grad_pre.astype(jnp.float32), 0)
    grad_norm_two = jnp.einsum("nf,df->nd", grad_pre, back_up, preferred_element_type=jnp.float32)
    grad_keys, grad_values = (
        lax.psum_scatter(keyed(grad_k_steps), "ctx", scatter_dimension=1, tiled=True),
        lax.psum_scatter(keyed(grad_v_steps), "ctx", scatter_dimension=1, tiled=True),
    )
    grad_queries = (
        grad_q_steps.reshape(seq_count, query_blocks, groups, step_rows, column_width)
        .transpose(0, 1, 3, 2, 4)
        .reshape(row_count, HEADS, HEAD)
    )
    grad_queries = turn(grad_queries, cosine, -sine_tab).reshape(row_count, model_width)
    grad_keys = turn(grad_keys.reshape(row_count, HEADS, HEAD), cosine, -sine_tab).reshape(
        row_count, model_width
    )
    grad_proj = jnp.concatenate(
        [grad_queries, grad_keys, grad_values.reshape(row_count, model_width)], 1
    ).astype(jnp.bfloat16)
    grad_qkv = jnp.einsum("nd,ne->de", normed_one, grad_proj, preferred_element_type=jnp.float32)
    grad_qkv_bias = jnp.sum(grad_proj.astype(jnp.float32), 0)
    grad_norm_one = jnp.einsum("ne,de->nd", grad_proj, back_qkv, preferred_element_type=jnp.float32)
    zero_bias = jnp.zeros((model_width,), jnp.float32)
    norm_one_pull = jax.vjp(layer_norm, inputs, back_gain_one.astype(jnp.float32), zero_bias)[1]
    grad_in_one, grad_gain_one, grad_bias_one = norm_one_pull(grad_norm_one)
    norm_two_pull = jax.vjp(layer_norm, inputs, back_gain_two.astype(jnp.float32), zero_bias)[1]
    grad_in_two, grad_gain_two, grad_bias_two = norm_two_pull(grad_norm_two)
    grad_inputs = (upstream_f + grad_in_one + grad_in_two).reshape(
        seq_count, local_rows, model_width
    )
    grads = (
        grad_gain_one,
        grad_bias_one,
        grad_gain_two,
        grad_bias_two,
        grad_qkv,
        grad_qkv_bias,
        grad_out,
        grad_out_bias,
        grad_up,
        grad_up_bias,
        grad_down,
        grad_out_bias,
    )
    shards = (
        lax.psum_scatter(grads[0], "fsdp", scatter_dimension=0, tiled=True),
        lax.psum_scatter(grads[1], "fsdp", scatter_dimension=0, tiled=True),
        lax.psum_scatter(grads[2], "fsdp", scatter_dimension=0, tiled=True),
        lax.psum_scatter(grads[3], "fsdp", scatter_dimension=0, tiled=True),
        lax.psum_scatter(grads[4], "fsdp", scatter_dimension=0, tiled=True),
        lax.psum_scatter(grads[5], "fsdp", scatter_dimension=0, tiled=True),
        lax.psum_scatter(grads[6], "fsdp", scatter_dimension=0, tiled=True),
        lax.psum_scatter(grads[7], "fsdp", scatter_dimension=0, tiled=True),
        lax.psum_scatter(grads[8], "fsdp", scatter_dimension=0, tiled=True),
        lax.psum_scatter(grads[9], "fsdp", scatter_dimension=0, tiled=True),
        lax.psum_scatter(grads[10], "fsdp", scatter_dimension=0, tiled=True),
        lax.psum_scatter(grads[11], "fsdp", scatter_dimension=0, tiled=True),
    )
    shards = lax.psum(
        (
            shards[0],
            shards[1],
            shards[2],
            shards[3],
            shards[4],
            shards[5],
            shards[6],
            shards[7],
            shards[8],
            shards[9],
            shards[10],
            shards[11],
        ),
        ("rep", "ctx"),
    )
    return (result, grad_inputs) + tuple(shards)


def solution(mesh):
    in_specs = (
        P(("rep", "fsdp"), "ctx", None),
        P(("rep", "fsdp"), None),
        P("fsdp"),
        P("fsdp"),
        P("fsdp"),
        P("fsdp"),
        P("fsdp", None),
        P("fsdp"),
        P("fsdp", None),
        P("fsdp"),
        P("fsdp", None),
        P("fsdp"),
        P("fsdp", None),
        P("fsdp"),
        P(("rep", "fsdp"), "ctx", None),
    )
    out_specs = (
        P(("rep", "fsdp"), "ctx", None),
        P(("rep", "fsdp"), "ctx", None),
        P("fsdp"),
        P("fsdp"),
        P("fsdp"),
        P("fsdp"),
        P("fsdp", None),
        P("fsdp"),
        P("fsdp", None),
        P("fsdp"),
        P("fsdp", None),
        P("fsdp"),
        P("fsdp", None),
        P("fsdp"),
    )
    return jax.shard_map(body, mesh=mesh, in_specs=in_specs, out_specs=out_specs, check_vma=False)
```

profile of v0, /device:TPU:0, one launch (start us, length us, event | category | flops | bytes accessed | tf_op | source)
XLA Modules:
  0.0 1386.1 jit_solution(12468133962966091920)
XLA Ops:
  9.4 6.1 all-gather.3
  16.2 5.3 all-gather.2
  22.2 5.1 all-gather.1
  30.9 27.8 %all-gather.15.cloned.1.call-done = bf16[1024,3072]{1,0:T(8,128)(2,1)} async-done(((bf16[256,3072]{1,0:T(8,128)(2,1)}), bf16[1024,3072]{1,0:T(8,128)(2,1)}) %all-gather.15.cloned.1.call-update) | async-done | bytes 6291472 | tf_op jit(solution)/shard_map/all_gather | solution.py:128
  58.7 5.8 convolution_add_fusion
  64.6 2.6 copy-done.4
  69.0 2.6 fusion.72
  72.4 4.0 fusion.91
  76.4 2.9 copy.42
  85.4 3.9 fusion.60
  91.9 26.3 %all-gather.25.cloned.1.call-done = bf16[1024,1024]{1,0:T(8,128)(2,1)} async-done(((bf16[512,1024]{1,0:T(8,128)(2,1)}), bf16[1024,1024]{1,0:T(8,128)(2,1)}) %all-gather.25.cloned.1.call-update) | async-done | bytes 2097168 | tf_op jit(solution)/shard_map/all_gather | solution.py:161
  118.2 3.1 copy.44
  121.3 31.5 %all-gather.17.cloned.1.call-done = bf16[1,1024,1024]{1,2,0:T(8,128)(2,1)} async-done(((bf16[1,512,1024]{1,2,0:T(8,128)(2,1)}), bf16[1,1024,1024]{1,2,0:T(8,128)(2,1)}) %all-gather.17.cloned.1.call-update) | async-done | bytes 2097168 | tf_op jit(solution)/shard_map/all_gather | solution.py:160
  152.8 58.9 %while.34 = (s32[]{:T(128)}, bf16[4,512,4,64]{1,3,2,0:T(8,128)(2,1)S(1)}, f32[4,4,512]{2,1,0:T(4,128)S(1)}, s32[4]{0:T(128)S(1)}, bf16[1,1024,1024]{1,2,0:T(8,12...) while((s32[]{:T(128)}, ...), condition=%wide.region_5.6_spmd.clone.clone, body=%wide.region_2.5_spmd.clone.sunk.clone | while | flops 562584576 | bytes 31795524 | solution.py:196
  156.4 2.6 fusion.169
  162.1 2.3 fusion.171
  164.4 3.0 fusion.172
  171.1 2.6 fusion.169
  179.1 3.0 fusion.172
  185.9 2.6 fusion.169
  193.9 3.0 fusion.172
  200.6 2.6 fusion.169
  208.6 3.0 fusion.172
  212.6 111.1 %while.35 = (s32[]{:T(128)}, f32[4,512,4,64]{1,3,2,0:T(8,128)}, f32[4,1024,4,64]{1,3,2,0:T(8,128)}, f32[4,1024,4,64]{1,3,2,0:T(8,128)}, s32[4]{0:T(128)S(1)}, /*...) while((s32[]{:T(128)}, f32[4,512,4,64]{1,3,2,0:T(8,128)}, ...), condition=%wide.region_8.9_spmd.clone.clone, body=%wide.region_6.8_spmd.clone.sunk.clone | while | flops 1364089856 | bytes 114870744 | solution.py:249
  217.6 4.6 fusion.183
  224.4 2.6 fusion.184
  227.4 6.2 multiply_reduce_fusion.3
  245.3 4.6 fusion.183
  252.2 2.6 fusion.184
  255.2 6.2 multiply_reduce_fusion.3
  273.1 4.6 fusion.183
  279.9 2.6 fusion.184
  282.9 6.2 multiply_reduce_fusion.3
  300.9 4.6 fusion.183
  307.7 2.6 fusion.184
  310.7 6.2 multiply_reduce_fusion.3
  325.9 3.3 fusion.64
  331.5 46.7 %reduce-scatter.7.cloned.1.call-done = f32[1,512,1024]{1,2,0:T(8,128)} async-done(((f32[1,1024,1024]{1,2,0:T(8,128)}), f32[1,512,1024]{1,2,0:T(8,128)}) %reduce-scatter.7.cloned.1.call-update) | async-done | bytes 2097168 | tf_op jit(solution)/shard_map/reduce_scatter | solution.py:264
  382.4 52.9 %reduce-scatter.9.cloned.1.call-done = f32[1,512,1024]{1,2,0:T(8,128)} async-done(((f32[1,1024,1024]{1,2,0:T(8,128)}), f32[1,512,1024]{1,2,0:T(8,128)}) %reduce-scatter.9.cloned.1.call-update) | async-done | bytes 2097168 | tf_op jit(solution)/shard_map/reduce_scatter | solution.py:265
  437.1 11.5 fusion.80
  449.3 5.2 all_gather.59
  454.5 5.1 all-gather.6
  459.5 5.1 all-gather.5
  464.6 30.7 %all-gather.21.cloned.1.call-done = bf16[1024,4096]{1,0:T(8,128)(2,1)} async-done(((bf16[256,4096]{1,0:T(8,128)(2,1)}), bf16[1024,4096]{1,0:T(8,128)(2,1)}) %all-gather.21.cloned.1.call-update) | async-done | bytes 8388624 | tf_op jit(solution)/shard_map/all_gather | solution.py:130
  495.3 27.6 %multiply_convert_fusion.1 = (bf16[512,4096]{1,0:T(8,128)(2,1)}, f32[512,4096]{1,0:T(8,128)}, f32[512,4096]{1,0:T(8,128)}) fusion(f32[4096]{0:T(1024)S(1)} %convert_element_type.144, bf16[1024,4096]{1,0:T(8,128)(2,1)} %all-gather.21.cloned.1.call-done, bf16[1,512,1024]{2,1,0:T(8,128)(2,1)S(1)} %copy-done.3, f32[1024]{0:T(1024)S(1)} %bitcast.360, ...), kind=kOutput, calls=%fused_computation.64 | convolution fusion | flops 4436525056 | bytes 30437376 | tf_op jit(solution)/shard_map/dot_general | solution.py:166
  522.9 32.3 %all-gather.23.cloned.1.call-done = bf16[4096,1024]{1,0:T(8,128)(2,1)} async-done(((bf16[1024,1024]{1,0:T(8,128)(2,1)}), bf16[4096,1024]{1,0:T(8,128)(2,1)}) %all-gather.23.cloned.1.call-update) | async-done | bytes 8388624 | tf_op jit(solution)/shard_map/all_gather | solution.py:206
  555.2 13.5 convert_reduce_fusion
  570.7 8.6 fusion.76
  579.6 12.8 fusion.62
  592.5 9.8 reduce-scatter.13.cloned.1.call-done
  602.3 101.7 %reduce-scatter.11.cloned.1.call-done = f32[256,3072]{1,0:T(8,128)} async-done(((f32[1024,3072]{1,0:T(8,128)}), f32[256,3072]{1,0:T(8,128)}) %reduce-scatter.11.cloned.1.call-update) | async-done | bytes 3145744 | tf_op jit(solution)/shard_map/reduce_scatter | solution.py:309
  703.9 128.9 %reduce-scatter.15.cloned.1.call-done = f32[256,4096]{1,0:T(8,128)} async-done(((f32[1024,4096]{1,0:T(8,128)}), f32[256,4096]{1,0:T(8,128)}) %reduce-scatter.15.cloned.1.call-update) | async-done | bytes 4194320 | tf_op jit(solution)/shard_map/reduce_scatter | solution.py:313
  832.9 128.6 %reduce-scatter.17.cloned.1.call-done = f32[1024,1024]{1,0:T(8,128)} async-done(((f32[4096,1024]{1,0:T(8,128)}), f32[1024,1024]{1,0:T(8,128)}) %reduce-scatter.17.cloned.1.call-update) | async-done | bytes 4194320 | tf_op jit(solution)/shard_map/reduce_scatter | solution.py:315
  962.1 5.1 all-gather.7
  967.2 5.1 all-gather.4
  974.8 8.3 fusion.94
  983.2 2.4 fusion.61
  985.6 7.3 fusion.95
  993.0 4.3 fusion.87
  1000.3 2.7 convert_reduce_fusion.2
  1003.0 11.7 all-reduce.9
  1015.1 39.7 %all-reduce.7 = (f32[256]{0:T(256)}, f32[256]{0:T(256)}, f32[256]{0:T(256)}, f32[256]{0:T(256)}, f32[768]{0:T(1024)}, /*index=5*/f32[256]{0:T(256)S(1)}, f32[1024]{0:T(1024)}) all-reduce(f32[256]{0:T(256)S(1)} %dynamic-slice.1, f32[256]{0:T(256)S(1)} %dynamic-slice.3, ...), channel_id=1, replica_groups=mesh['rep'=4,'fsdp'=4,'ctx'=2] {'rep','ctx'}, use_global_device_ids=true, to_apply=%region_17.18 | all-reduce | flops 3072 | bytes 24576 | tf_op jit(solution)/shard_map/psum | solution.py:318
  1054.8 313.3 %all-reduce.12.cloned.1.call-done = (f32[256,3072]{1,0:T(8,128)}, f32[256,1024]{1,0:T(8,128)}, f32[256,4096]{1,0:T(8,128)}, f32[1024,1024]{1,0:T(8,128)}) async-done(((f32[256,3072]{1,0:T(8,128)}, f32[256,1024]{1,0:T(8,128)}, f32[256,4096]{1,0:T(8,128)}, f32[1024,1024]{1,0:T(8,128)}), (f32[256,3072]{1,0:T(8,128)}, f32[256,1024]{1,0:T(8,128)}, f32[256,4096]{1,0:T(8,128)}, ...) | async-done | bytes 12582928 | tf_op jit(solution)/shard_map/psum | solution.py:318
  1368.7 4.0 copy.85
  (271 shorter events, 114.8 us)
Async XLA Ops:
  7.2 51.5 %copy-start.2 = (bf16[1,512,1024]{2,1,0:T(8,128)(2,1)S(1)}, bf16[1,512,1024]{2,1,0:T(8,128)(2,1)}, u32[]{:S(2)}) copy-start(bf16[1,512,1024]{2,1,0:T(8,128)(2,1)} %param.19) | copy-start | bytes 3145732
  7.2 51.5 %all-gather.15.cloned.1.call-start = ((), (), s32[]{:S(2)}) async-start(), calls=%async_computation.6 | async-start | bytes 7864320 | tf_op jit(solution)/shard_map/all_gather | solution.py:128
  7.9 77.5 %all-gather.19.cloned.1.call-start = ((), (), s32[]{:S(2)}) async-start(), calls=%async_computation.8 | async-start | bytes 2621440 | tf_op jit(solution)/shard_map/all_gather | solution.py:204
  8.7 109.5 %all-gather.25.cloned.1.call-start = ((), (), s32[]{:S(2)}) async-start(), calls=%async_computation.17 | async-start | bytes 3145728 | tf_op jit(solution)/shard_map/all_gather | solution.py:161
  21.5 43.0 %copy-start.27 = (f32[4,1,256]{2,1,0:T(1,128)}, f32[4,1,256]{2,1,0:T(1,128)S(1)}, u32[]{:S(2)}) copy-start(f32[4,1,256]{2,1,0:T(1,128)S(1)} %convert_element_type.154) | copy-start | bytes 12292
  27.2 37.3 %copy-start.18 = (f32[4,1,256]{2,1,0:T(1,128)}, f32[4,1,256]{2,1,0:T(1,128)S(1)}, u32[]{:S(2)}) copy-start(f32[4,1,256]{2,1,0:T(1,128)S(1)} %convert_element_type.153) | copy-start | bytes 12292
  28.7 35.8 %copy-start.20 = (f32[512]{0:T(512)}, f32[512]{0:T(512)S(1)}, u32[]{:S(2)}) copy-start(f32[512]{0:T(512)S(1)} %broadcast_multiply_fusion) | copy-start | bytes 6148
  30.9 33.6 %copy-start.22 = (f32[512]{0:T(512)}, f32[512]{0:T(512)S(1)}, u32[]{:S(2)}) copy-start(f32[512]{0:T(512)S(1)} %fusion.75) | copy-start | bytes 6148
  58.7 9.7 copy-start.26
  64.6 2.6 copy-start.4
  68.3 84.4 %all-gather.17.cloned.1.call-start = ((), (), s32[]{:S(2)}) async-start(), calls=%async_computation.7 | async-start | bytes 3145728 | tf_op jit(solution)/shard_map/all_gather | solution.py:160
  72.4 10.3 copy-start.15
  81.1 4.3 copy-start.8
  85.2 292.9 %reduce-scatter.7.cloned.1.call-start = ((), (), s32[]{:S(2)}) async-start(), calls=%async_computation.11 | async-start | bytes 6291456 | tf_op jit(solution)/shard_map/reduce_scatter | solution.py:264
  212.6 3.8 copy-start
  227.0 6.6 slice-start
  227.4 6.2 slice-start.1
  238.5 1.9 copy-start.1
  240.4 3.8 copy-start
  254.8 6.6 slice-start
  255.2 6.2 slice-start.1
  266.3 1.9 copy-start.1
  268.2 3.8 copy-start
  282.6 6.6 slice-start
  282.9 6.2 slice-start.1
  294.1 1.9 copy-start.1
  295.9 3.8 copy-start
  310.3 6.6 slice-start
  310.7 6.2 slice-start.1
  321.8 1.9 copy-start.1
  323.7 111.6 %reduce-scatter.9.cloned.1.call-start = ((), (), s32[]{:S(2)}) async-start(), calls=%async_computation.12 | async-start | bytes 6291456 | tf_op jit(solution)/shard_map/reduce_scatter | solution.py:265
  323.8 2.1 copy-start.9
  323.8 2.1 copy-start.13
  324.3 171.0 %all-gather.21.cloned.1.call-start = ((), (), s32[]{:S(2)}) async-start(), calls=%async_computation.9 | async-start | bytes 10485760 | tf_op jit(solution)/shard_map/all_gather | solution.py:130
  325.1 230.1 %all-gather.23.cloned.1.call-start = ((), (), s32[]{:S(2)}) async-start(), calls=%async_computation.10 | async-start | bytes 10485760 | tf_op jit(solution)/shard_map/all_gather | solution.py:206
  325.8 276.5 %reduce-scatter.13.cloned.1.call-start = ((), (), s32[]{:S(2)}) async-start(), calls=%async_computation.14 | async-start | bytes 5242880 | tf_op jit(solution)/shard_map/reduce_scatter | solution.py:311
  329.1 50.6 %copy-start.16 = (f32[512,8]{0,1:T(8,128)S(1)}, f32[512,8]{0,1:T(8,128)}, u32[]{:S(2)}) copy-start(f32[512,8]{0,1:T(8,128)} %copy-done.15) | copy-start | bytes 49156
  329.1 50.6 %copy-start.17 = (f32[512,8]{0,1:T(8,128)S(1)}, f32[512,8]{0,1:T(8,128)}, u32[]{:S(2)}) copy-start(f32[512,8]{0,1:T(8,128)} %get-tuple-element.545) | copy-start | bytes 49156
  329.2 374.8 %reduce-scatter.11.cloned.1.call-start = ((), (), s32[]{:S(2)}) async-start(), calls=%async_computation.13 | async-start | bytes 15728640 | tf_op jit(solution)/shard_map/reduce_scatter | solution.py:309
  379.7 57.3 %copy-start.3 = (bf16[1,512,1024]{2,1,0:T(8,128)(2,1)S(1)}, bf16[1,512,1024]{2,1,0:T(8,128)(2,1)}, u32[]{:S(2)}) copy-start(bf16[1,512,1024]{2,1,0:T(8,128)(2,1)} %param.19) | copy-start | bytes 3145732
  379.7 57.3 %copy-start.19 = (f32[4,1,256]{2,1,0:T(1,128)S(1)}, f32[4,1,256]{2,1,0:T(1,128)}, u32[]{:S(2)}) copy-start(f32[4,1,256]{2,1,0:T(1,128)} %copy-done.18) | copy-start | bytes 12292
  379.7 57.3 %copy-start.21 = (f32[512]{0:T(512)S(1)}, f32[512]{0:T(512)}, u32[]{:S(2)}) copy-start(f32[512]{0:T(512)} %copy-done.20) | copy-start | bytes 6148
  379.8 57.3 %copy-start.23 = (f32[512]{0:T(512)S(1)}, f32[512]{0:T(512)}, u32[]{:S(2)}) copy-start(f32[512]{0:T(512)} %copy-done.22) | copy-start | bytes 6148
  379.8 57.3 %copy-start.28 = (f32[4,1,256]{2,1,0:T(1,128)S(1)}, f32[4,1,256]{2,1,0:T(1,128)}, u32[]{:S(2)}) copy-start(f32[4,1,256]{2,1,0:T(1,128)} %copy-done.27) | copy-start | bytes 12292
  448.6 5.9 copy-start.32
  448.6 11.0 copy-start.33
  448.6 384.2 %reduce-scatter.15.cloned.1.call-start = ((), (), s32[]{:S(2)}) async-start(), calls=%async_computation.15 | async-start | bytes 20971520 | tf_op jit(solution)/shard_map/reduce_scatter | solution.py:313
  568.7 2.0 copy-start.37
  579.4 382.1 %reduce-scatter.17.cloned.1.call-start = ((), (), s32[]{:S(2)}) async-start(), calls=%async_computation.16 | async-start | bytes 20971520 | tf_op jit(solution)/shard_map/reduce_scatter | solution.py:315
  592.4 775.7 %all-reduce.12.cloned.1.call-start = ((), (), s32[]{:S(2)}) async-start(), calls=%async_computation.18 | async-start | bytes 25165824 | tf_op jit(solution)/shard_map/psum | solution.py:318
  961.4 5.7 copy-start.35
  961.5 10.8 copy-start.36
  974.8 8.3 copy-start.14
  974.8 8.3 copy-start.31
  983.1 2.5 copy-start.38
  983.1 9.8 slice-start.2
  985.6 7.4 copy-start.7
  985.6 7.4 slice-start.3
  993.0 4.3 copy-start.25
  997.3 3.0 copy-start.10
  1054.8 318.9 %copy-start.30 = (f32[256]{0:T(256)}, f32[256]{0:T(256)S(1)}, u32[]{:S(2)}) copy-start(f32[256]{0:T(256)S(1)} %get-tuple-element.934) | copy-start | bytes 3076
  1368.1 4.6 copy-start.11
  1368.7 5.0 copy-start.6
  1373.7 3.7 copy-start.5
  (4 other events, 2.9 us)
Sparse Core Ops, SparseCore 0:
  9.6 49.0 all-gather.14
  60.3 22.5 all-gather.18
  85.0 33.1 all-gather.24
  119.6 33.1 all-gather.16
  323.8 54.2 reduce-scatter.6
  381.0 54.2 reduce-scatter.8
  436.9 58.3 all-gather.20
  496.9 58.2 all-gather.22
  557.7 44.4 reduce-scatter.12
  604.9 99.0 reduce-scatter.10
  706.7 126.0 reduce-scatter.14
  835.3 126.1 reduce-scatter.16
  966.9 401.1 all-reduce.11
where the time goes:
time: 1390 us
  waiting for transfers between devices  934 us (67%)
  matrix products  195 us (14%)
  blocking collectives  93.2 us (7%)
  local copies, waits for them, and re-layouts  68.2 us (5%)
  other arithmetic  56.8 us (4%)
  loops' own time  21.7 us (2%)
  between operations  16.7 us (1%)
    psum x1, waiting for transfers between devices, body(): lax.psum((shards[0], shards[1], shards[2], shards[3], shards[4], shards[5...  313 us
    reduce_scatter x1, waiting for transfers between devices, body(): lax.psum_scatter(grads[8], 'fsdp', scatter_dimension=0, tiled=True)  129 us
    reduce_scatter x1, waiting for transfers between devices, body(): lax.psum_scatter(grads[10], 'fsdp', scatter_dimension=0, tiled=True)  129 us
    reduce_scatter x1, waiting for transfers between devices, body(): lax.psum_scatter(grads[4], 'fsdp', scatter_dimension=0, tiled=True)  102 us
    reduce_scatter x1, waiting for transfers between devices, body(): lax.psum_scatter(keyed(grad_v_steps), 'ctx', scatter_dimension=1, tiled=T...  52.9 us
    reduce_scatter x1, waiting for transfers between devices, body(): lax.psum_scatter(keyed(grad_k_steps), 'ctx', scatter_dimension=1, tiled=T...  46.7 us
    psum x1, blocking collectives, body(): lax.psum((shards[0], shards[1], shards[2], shards[3], shards[4], shards[5...  39.7 us
    all_gather x1, waiting for transfers between devices, body(): lax.all_gather(w_down, 'fsdp', axis=0, tiled=True)  32.3 us
  transfers between devices with their start and end apart: 13, of which 12 were waited for; matrix products, arithmetic and copies ran while one was open for 11% of the time, Pallas kernels for 0%

commit v1 on v0

v1 whole, which is shorter than its diff:
```python
import functools
import math

import jax
import jax.numpy as jnp
from jax import lax
from jax.experimental import pallas as pl
from jax.experimental.pallas import tpu as pltpu
from jax.sharding import PartitionSpec as P

HEADS = 16
HEAD = 64
ROT = 16
BLK = 256
EPSILON = 1e-05
CW = 512
HW = CW // 2
TT = 256
SLOTS = 4
LINK = pl.DeviceIdType.MESH
BF = jnp.bfloat16
F32 = jnp.float32

NN = (((1,), (0,)), ((), ()))
NT = (((1,), (1,)), ((), ()))
TN = (((0,), (0,)), ((), ()))


def mm(a, b, dims=NN):
    return lax.dot_general(a, b, dims, preferred_element_type=F32)


def mult(value, of):
    return value if isinstance(value, int) else pl.multiple_of(value, of)


def kernel(
    dims,
    x_ref,
    g_ref,
    oh_ref,
    sm_ref,
    wqkv_ref,
    wo_ref,
    wup_ref,
    wdn_ref,
    tab_ref,
    fin_up,
    fin_dn,
    fin_qkv,
    fin_o,
    out_ref,
    gin_ref,
    sg_ref,
    gbuf,
    xrecv,
    ar,
    af,
    mo,
    X3,
    G3,
    wup,
    wdn,
    wqkv,
    wo,
    oh_v,
    sm_v,
    vecs,
    sgv,
    sgA,
    sgB,
    own,
    yrecv,
    zin,
    zback,
    ysend,
    st,
    tot,
    sems,
):
    X, NREP, R, D, FF = dims
    L = 2 * R
    RX = D // X
    RS = D // (2 * X)
    SW = CW // X
    NJ = FF // 2 // CW
    NB = L // TT
    NP = 2 * NJ + 4
    h = NREP // 2

    f = lax.axis_index("fsdp")
    y = lax.axis_index("ctx")
    r = lax.axis_index("rep")
    c = lax.rem(f, 2)
    xi = lax.div(f, 2)
    fs = xi * 2 + (1 - c)
    yo = 1 - y

    counter = [0]

    def S():
        counter[0] += 1
        return counter[0] - 1

    def rcopy(src, dst, ss, rs, **dev):
        cp = pltpu.make_async_remote_copy(
            src_ref=src,
            dst_ref=dst,
            send_sem=sems.at[ss],
            recv_sem=sems.at[rs],
            device_id=dev,
            device_id_type=LINK,
        )
        cp.start()
        return cp

    def lcopy(src, dst, s):
        cp = pltpu.make_async_copy(src, dst, sems.at[s])
        cp.start()
        return cp

    def wait(s, ref):
        pltpu.make_async_copy(ref, ref, sems.at[s]).wait()

    finals = []

    NG = NJ + 2
    gxs = [S() for _ in range(NG)]
    gxr = [S() for _ in range(NG)]
    gzs = [S() for _ in range(NG)]
    gzr = [S() for _ in range(NG)]
    gcs = [S() for _ in range(NG)]
    gcr = [S() for _ in range(NG)]
    gl = [S() for _ in range(NG)]
    q = lax.rem(r, 2)
    zp = r + 1 - 2 * q

    def cols(k, ct):
        if k < NJ:
            for xx in range(X):
                yield (
                    wup_ref,
                    mult((FF // X) * xx + (FF // (2 * X)) * ct + SW * k, 128),
                    wup.at[k],
                    xx * SW,
                )
        elif k == NJ:
            for m in range(3):
                for xx in range(X):
                    yield (
                        wqkv_ref,
                        mult(D * m + (D // X) * xx + SW * ct, 128),
                        wqkv,
                        m * CW + xx * SW,
                    )

    def rows_of(k):
        if k < NJ:
            return (wdn_ref, SW * k, wdn.at[k])
        if k == NJ + 1:
            return (wo_ref, 0, wo)
        return None

    def part(ref, row, n, col, w):
        return ref.at[pl.ds(row, n), pl.ds(col, w)]

    def span(ref, row, n):
        return ref.at[pl.ds(row, n)]

    def xz_bytes(k):
        if k < NJ:
            return gbuf.at[0, pl.ds(0, X - 1)]
        if k == NJ:
            return xrecv.at[pl.ds(0, 3), :, pl.ds(0, RX // 2)]
        return gbuf.at[0, pl.ds(0, X - 1), pl.ds(0, RX // 2)]

    def gather_x(k):
        n = RS // 2
        r0 = mult(q * n, n)
        for dx in range(1, X):
            xo = lax.rem(xi + dx, X)
            for ct in range(2):
                for src, sc, dst, dc in cols(k, ct):
                    rcopy(
                        part(src, r0, n, sc, SW),
                        part(dst, mult(RS * f + r0, n), n, dc, SW),
                        gxs[k],
                        gxr[k],
                        fsdp=2 * xo + ct,
                    )
            rw = rows_of(k)
            if rw is not None:
                src, sr, dst = rw
                rcopy(
                    span(src, mult(sr + r0, n), n),
                    span(dst, mult(xi * SW + r0, n), n),
                    gxs[k],
                    gxr[k],
                    fsdp=2 * xo + c,
                )
        finals.append(lambda: wait(gxs[k], xz_bytes(k)))

    def gather_fwd(k):
        wait(gxr[k], xz_bytes(k))
        n = RS // 2
        r0 = mult(q * n, n)
        dst = wup.at[k] if k < NJ else wqkv
        for dx in range(1, X):
            xo = lax.rem(xi + dx, X)
            if k <= NJ:
                for ct in range(2):
                    piece = span(dst, mult(RS * (2 * xo + ct) + r0, n), n)
                    rcopy(piece, piece, gzs[k], gzr[k], rep=zp)
            rw = rows_of(k)
            if rw is not None:
                piece = span(rw[2], mult(xo * SW + r0, n), n)
                rcopy(piece, piece, gzs[k], gzr[k], rep=zp)
        finals.append(lambda: wait(gzs[k], xz_bytes(k)))

    def core_bytes(k):
        if k < NJ:
            return gbuf.at[0, 0, pl.ds(0, RX // 2)]
        return gbuf.at[pl.ds(0, 3), 0, pl.ds(0, RX // 2)]

    def local_bytes(k):
        n = 2 if k == NJ + 1 else 3
        return gbuf.at[pl.ds(0, n), 0, pl.ds(0, RX // 2)]

    def gather_core(k):
        for src, sc, dst, dc in cols(k, 1 - c):
            rcopy(
                part(src, 0, RS, sc, SW),
                part(dst, mult(RS * f, RS), RS, dc, SW),
                gcs[k],
                gcr[k],
                fsdp=fs,
            )
        for src, sc, dst, dc in cols(k, c):
            lcopy(part(src, 0, RS, sc, SW), part(dst, mult(RS * f, RS), RS, dc, SW), gl[k])
        rw = rows_of(k)
        if rw is not None:
            src, sr, dst = rw
            lcopy(span(src, sr, SW), span(dst, mult(xi * SW, SW), SW), gl[k])
        if k <= NJ:
            finals.append(lambda: wait(gcs[k], core_bytes(k)))

    def gather_wait(k):
        wait(gl[k], local_bytes(k))
        if k <= NJ:
            wait(gcr[k], core_bytes(k))
        wait(gzr[k], xz_bytes(k))

    xs = [S() for _ in range(NP)]
    xr = [S() for _ in range(NP)]
    ys = [S() for _ in range(NP)]
    yr = [S() for _ in range(NP)]
    zis = [S() for _ in range(NP)]
    zir = [S() for _ in range(NP)]
    zbs = [S() for _ in range(NP)]
    zbr = [S() for _ in range(NP)]
    ags = [S() for _ in range(NP)]
    agr = [S() for _ in range(NP)]
    agl = [S() for _ in range(NP)]
    stl = S()
    lp = S()
    m = jnp.where(r < h, r, NREP - 1 - r)
    inner = jnp.where(r < h, r + 1, r - 1)
    outer = jnp.where(r < h, r - 1, r + 1)

    def is_up(p):
        return (p < 2 * NJ and p % 2 == 0) or p > 2 * NJ

    def x_bytes():
        return gbuf.at[0, pl.ds(0, X - 1)]

    def send_x(p):
        for dx in range(1, X):
            xo = lax.rem(xi + dx, X)
            rcopy(gbuf.at[p, xo], xrecv.at[p, dx - 1], xs[p], xr[p], fsdp=2 * xo + c)
        finals.append(lambda: wait(xs[p], x_bytes()))

    def add_rows(count, fn):
        def step(i, carry):
            fn(pl.ds(mult(i * 64, 64), 64))
            return carry

        lax.fori_loop(0, count // 64, step, 0)

    def stage_x(p):
        wait(xr[p], x_bytes())
        for side, half in ((0, yo), (1, y)):
            at = pl.ds(mult(half * HW, HW), HW)
            lcopy(gbuf.at[p, xi, :, at], st.at[side], stl)
            for d in range(X - 1):
                lcopy(xrecv.at[p, d, :, at], st.at[2 + 2 * d + side], stl)
        slot = p % SLOTS
        if p >= SLOTS:
            wait(ys[p - SLOTS], ysend.at[0])
        wait(stl, gbuf.at[0])

        def add(rows):
            for side in range(2):
                total = st[side, rows, :].astype(F32)
                for d in range(X - 1):
                    total = total + st[2 + 2 * d + side, rows, :].astype(F32)
                if side == 0:
                    ysend[slot, rows, :] = total.astype(BF)
                else:
                    own[p, rows, :] = total.astype(BF)

        add_rows(RX, add)
        rcopy(ysend.at[slot], yrecv.at[p], ys[p], yr[p], ctx=yo)

    def send_in(p, at_middle):
        if at_middle:
            rcopy(own.at[p], zback.at[p], zis[p], zbr[p], rep=inner)
        else:
            rcopy(own.at[p], zin.at[p], zis[p], zir[p], rep=inner)

    def add_into(p, dst, other):
        def add(rows):
            dst[p, rows, :] = (own[p, rows, :].astype(F32) + other[p, rows, :].astype(F32)).astype(
                BF
            )

        add_rows(RX, add)

    def stage_y(p):
        wait(yr[p], own.at[0])
        add_into(p, own, yrecv)

        @pl.when(m == 0)
        def _():
            send_in(p, h == 1)

        finals.append(lambda: wait(zis[p], own.at[0]))

    def stage_in(k, p):
        @pl.when(m == k)
        def _():
            wait(zir[p], own.at[0])
            add_into(p, own, zin)
            send_in(p, k == h - 1)

    def stage_out(i, p):
        @pl.when(m == h - 1 - i)
        def _():
            wait(zbr[p], own.at[0])
            if i == 0:
                add_into(p, zback, zback)
            if h - 1 - i > 0:
                rcopy(zback.at[p], zback.at[p], zbs[p], zbr[p], rep=outer)

    def ag_bytes(p):
        return own.at[pl.ds(0, 3), pl.ds(0, RS)] if is_up(p) else own.at[0]

    def stage_ag(p):
        for i in range(X // 2):
            b = y * (X // 2) + i
            lanes = pl.ds(i * SW, SW)
            if is_up(p):
                if p < 2 * NJ:
                    dst, base, whole = fin_up, SW * (p // 2), FF
                else:
                    dst, base, whole = fin_qkv, D * (p - 2 * NJ - 1), D
                at = mult(base + (whole // X) * b + (whole // (2 * X)) * c, 128)
                mine = zback.at[p, pl.ds(mult(c * RS, RS), RS), lanes]
                theirs = zback.at[p, pl.ds(mult((1 - c) * RS, RS), RS), lanes]
                to = dst.at[:, pl.ds(at, SW)]
                lcopy(mine, to, agl[p])
                rcopy(theirs, to, ags[p], agr[p], fsdp=fs)
                rcopy(mine, to, ags[p], agr[p], ctx=yo)
                rcopy(theirs, to, ags[p], agr[p], fsdp=fs, ctx=yo)
            else:
                dst, base = (fin_dn, SW * (p // 2)) if p < 2 * NJ else (fin_o, 0)
                src = zback.at[p, :, lanes]
                to = dst.at[pl.ds(mult(b * RX, RX), RX), pl.ds(base, SW)]
                lcopy(src, to, agl[p])
                rcopy(src, to, ags[p], agr[p], ctx=yo)
        finals.append(lambda: wait(agl[p], own.at[0, pl.ds(0, RS)] if is_up(p) else own.at[0]))
        finals.append(lambda: wait(ags[p], ag_bytes(p)))
        finals.append(lambda: wait(agr[p], ag_bytes(p)))

    stages = [stage_x, stage_y]
    for k in range(1, h):
        stages.append(functools.partial(stage_in, k))
    for i in range(h):
        stages.append(functools.partial(stage_out, i))
    stages.append(stage_ag)
    live = []
    waiting = []

    def tick():
        for item in list(live):
            p, s = item
            stages[s](p)
            if s == len(stages) - 2:
                stages[s + 1](p)
                live.remove(item)
            else:
                item[1] = s + 1
        if waiting:
            p = waiting.pop(0)
            stages[0](p)
            live.append([p, 1])

    def grad_piece(p, lhs_t, rhs, gst):
        per = RX // TT

        def step(t, carry):
            b = lax.div(t, per)
            row = pl.ds(mult(lax.rem(t, per) * TT, TT), TT)
            res = mm(lhs_t[pl.ds(mult(t * TT, TT), TT), :], rhs()).astype(BF)
            if is_up(p):
                gst[b, row, :] = res
            else:
                for xx in range(X):
                    gst[xx, row, pl.ds(mult(b * SW, 128), SW)] = res[:, xx * SW : (xx + 1) * SW]
            return carry

        lax.fori_loop(0, D // TT, step, 0)
        lcopy(gst, gbuf.at[p], lp).wait()
        send_x(p)
        waiting.append(p)

    bar = pltpu.get_barrier_semaphore()
    near = []
    for df in range(2 * X):
        for dy in range(2):
            if df or dy:
                near.append(dict(fsdp=lax.rem(f + df, 2 * X), ctx=lax.rem(y + dy, 2)))
    for dr in range(1, NREP):
        near.append(dict(rep=lax.rem(r + dr, NREP)))
    for dev in near:
        pl.semaphore_signal(bar, inc=1, device_id=dev, device_id_type=LINK)
    pl.semaphore_wait(bar, len(near))

    gather_core(0)
    gather_x(0)
    s_sm, r_sm, l_sm = S(), S(), S()
    lcopy(sm_ref, sm_v.at[f], l_sm)
    for df in range(1, 2 * X):
        rcopy(sm_ref, sm_v.at[f], s_sm, r_sm, fsdp=lax.rem(f + df, 2 * X))
    s_bo, r_bo, l_bo = S(), S(), S()
    lcopy(oh_ref, oh_v.at[c], l_bo)
    rcopy(oh_ref, oh_v.at[c], s_bo, r_bo, fsdp=fs)
    tok = []
    for src, dst in ((x_ref, X3), (g_ref, G3)):
        ids = [S() for _ in range(7)]
        lcopy(src, dst.at[c], ids[0])
        rcopy(src, dst.at[c], ids[1], ids[2], fsdp=fs)
        tok.append((src, dst, ids))
    gather_x(1)
    for src, dst, ids in tok:

        @pl.when(c != y)
        def _():
            rcopy(src, dst.at[2], ids[3], ids[4], ctx=yo)

    for k in range(1, NG):
        gather_core(k)

    def exchange_forward():
        for src, dst, ids in tok:

            @pl.when(c == y)
            def _():
                wait(ids[4], dst.at[2])
                rcopy(dst.at[2], dst.at[2], ids[5], ids[6], fsdp=fs)

    def exchange_finish():
        for src, dst, ids in tok:

            @pl.when(c != y)
            def _():
                wait(ids[6], dst.at[2])
                wait(ids[3], src)

            @pl.when(c == y)
            def _():
                wait(ids[5], dst.at[2])

    wait(l_sm, sm_ref)
    wait(r_sm, sm_v.at[pl.ds(0, 2 * X - 1)])
    for ff in range(2 * X):
        vecs[:, ff * RS : (ff + 1) * RS] = sm_v[ff]
    sgv[...] = jnp.zeros_like(sgv)
    for src, dst, ids in tok:
        wait(ids[0], dst.at[0])
        wait(ids[2], dst.at[0])

    def vec(row):
        return vecs[row : row + 1, :]

    def center(blk):
        v = blk.astype(F32)
        mid = v - jnp.mean(v, -1, keepdims=True)
        rs = lax.rsqrt(jnp.mean(mid * mid, -1, keepdims=True) + EPSILON)
        return mid * rs, rs

    def norm_back(e, blk, gain, row):
        n, rs = center(blk)
        sgv[row : row + 1, :] += jnp.sum(e * n, 0, keepdims=True)
        sgv[row + 1 : row + 2, :] += jnp.sum(e, 0, keepdims=True)
        eg = e * gain
        return rs * (
            eg - jnp.mean(eg, -1, keepdims=True) - n * jnp.mean(eg * n, -1, keepdims=True)
        )

    def ds(i, size=TT):
        return pl.ds(mult(i * size, size), size)

    s_mo = [S() for _ in range(2)]
    r_mo = [S() for _ in range(2)]

    def feed(n2, n2t, gt, acc_o, acc_g, hid, gup, gst):
        def prep(b, carry):
            half, row = lax.div(b, NB // 2), ds(lax.rem(b, NB // 2))
            n, _ = center(X3[half, row, :])
            v = (n * vec(2) + vec(3)).astype(BF)
            n2[ds(b), :] = v
            n2t[:, ds(b)] = v.T
            gt[:, ds(b)] = G3[half, row, :].T
            return carry

        lax.fori_loop(0, NB, prep, 0)

        def gsum(b, carry):
            sgv[4:5, :] += jnp.sum(G3[c, ds(b), :].astype(F32), 0, keepdims=True)
            return carry

        lax.fori_loop(0, NB // 2, gsum, 0)
        gather_fwd(0)
        gather_x(2)
        gather_fwd(1)
        gather_x(3)
        exchange_forward()
        for j in range(NJ):
            gather_wait(j)
            bias = jnp.concatenate(
                [vecs[8 + j : 9 + j, ds(2 * xx + c, RS)] for xx in range(X)], 1
            )

            def tile(t, gb):
                half, row = lax.div(t, NB // 2), ds(lax.rem(t, NB // 2))
                g = G3[half, row, :]
                up = mm(n2[ds(t), :], wup[j]) + bias
                cdf = 0.5 + 0.5 * lax.erf(up * (1.0 / math.sqrt(2.0)))
                hd = (up * cdf).astype(BF)
                hid[ds(t), :] = hd
                gh = mm(g, wdn[j], NT)
                pdf = jnp.exp(-0.5 * up * up) * (1.0 / math.sqrt(2.0 * math.pi))
                gu = (gh * (cdf + up * pdf)).astype(BF)
                gup[ds(t), :] = gu
                o = mm(hd, wdn[j])
                gn = mm(gu, wup[j], NT)
                if j == 0:
                    acc_o[ds(t), :] = o
                    acc_g[ds(t), :] = gn
                else:
                    acc_o[ds(t), :] += o
                    acc_g[ds(t), :] += gn
                return gb + jnp.sum(gu.astype(F32), 0, keepdims=True)

            gb = lax.fori_loop(0, NB, tile, jnp.zeros((1, CW), F32))
            for xx in range(X):
                sgv[5 + j : 6 + j, ds(2 * xx + c, RS)] = gb[:, xx * SW : (xx + 1) * SW]
            grad_piece(2 * j, n2t, lambda: gup[...], gst)
            grad_piece(2 * j + 1, gt, lambda: hid[...], gst)
            if j + 2 < NG:
                gather_fwd(j + 2)
            if j + 4 < NG:
                gather_x(j + 4)

        def give(i, carry):
            b = (1 - c) * (NB // 2) + i
            n2[ds(i), :] = acc_o[ds(b), :].astype(BF)
            e = norm_back(acc_g[ds(b), :], X3[1 - c, ds(i), :], vec(2), 2)
            n2[ds(i + NB // 2), :] = e.astype(BF)
            return carry

        lax.fori_loop(0, NB // 2, give, 0)
        sends = [rcopy(n2.at[pl.ds(a * R, R)], mo.at[a], s_mo[a], r_mo[a], fsdp=fs) for a in range(2)]

        def keep(i, carry):
            b = c * (NB // 2) + i
            xb = X3[c, ds(i), :]
            o = acc_o[ds(b), :] + xb.astype(F32) + vec(7) + vec(12)
            tot[0, ds(i), :] = o.astype(BF)
            e = norm_back(acc_g[ds(b), :], xb, vec(2), 2)
            tot[1, ds(i), :] = (e + G3[c, ds(i), :].astype(F32)).astype(BF)
            return carry

        lax.fori_loop(0, NB // 2, keep, 0)
        for cp in sends:
            cp.wait_send()

    pl.run_scoped(
        feed,
        pltpu.VMEM((L, D), BF),
        pltpu.VMEM((D, L), BF),
        pltpu.VMEM((D, L), BF),
        pltpu.VMEM((L, D), F32),
        pltpu.VMEM((L, D), F32),
        pltpu.VMEM((L, CW), BF),
        pltpu.VMEM((L, CW), BF),
        pltpu.VMEM((X, RX, CW), BF),
    )

    s_ar = [S() for _ in range(2)]
    r_ar = [S() for _ in range(2)]
    s_af = [S() for _ in range(2)]
    r_af = [S() for _ in range(2)]
    l_af = [S() for _ in range(2)]
    l_tab, l_st = S(), S()

    def attend(n1, n1t, gs, gst_t, qkv, ctx, gctx, gproj, dkv, tab, gst, stage):
        lcopy(tab_ref, tab, l_tab)
        wait(l_bo, oh_ref)
        wait(r_bo, oh_ref)
        exchange_finish()

        def weight(b, s, width):
            w = oh_v[y, pl.ds(b * NB + s, 1), :].astype(BF)
            return jnp.concatenate([w] * (width // 128), 1)

        def place(s):
            half = s // (NB // 2) if isinstance(s, int) else lax.div(s, NB // 2)
            row = s % (NB // 2) if isinstance(s, int) else lax.rem(s, NB // 2)
            return jnp.where(half == y, y, 2), ds(row)

        def in_order(ref, b):
            total = None
            for s in range(NB):
                src, row = place(s)
                term = ref[src, row, :] * weight(b, s, D)
                total = term if total is None else total + term
            return total

        def in_slot(ref, s, width):
            total = None
            for b in range(NB):
                term = ref[b * TT : (b + 1) * TT, :] * weight(b, s, width)
                total = term if total is None else total + term
            return total

        def prep(b, carry):
            n, _ = center(in_order(X3, b))
            v = (n * vec(0) + vec(1)).astype(BF)
            n1[ds(b), :] = v
            n1t[:, ds(b)] = v.T
            gv = in_order(G3, b)
            gs[ds(b), :] = gv
            gst_t[:, ds(b)] = gv.T
            return carry

        lax.fori_loop(0, NB, prep, 0)
        wait(l_tab, tab_ref)
        tick()
        gather_wait(NJ)

        def turned(v, rows, sign):
            right = pltpu.roll(v, ROT // 2, 1)
            left = pltpu.roll(v, 128 - ROT // 2, 1)
            return v * tab[0, rows, :] + sign * (
                right * tab[1, rows, :] + left * tab[2, rows, :]
            )

        for mm_i in range(3):
            parts = []
            for xx in range(X):
                both = []
                for cc in range(2):
                    nb = 2 * X * mm_i + 2 * xx + cc
                    both.append(sm_v[nb // 3, 4 + nb % 3 : 5 + nb % 3, :])
                parts.append(jnp.where(c == 0, both[0], both[1]))
            bias = jnp.concatenate(parts, 1)

            def proj(t, carry):
                v = mm(n1[ds(t), :], wqkv[:, mm_i * CW : (mm_i + 1) * CW]) + bias
                if mm_i == 2:
                    qkv[2, ds(t), :] = v.astype(BF)
                else:
                    for u in range(CW // 128):
                        w = turned(v[:, u * 128 : (u + 1) * 128], ds(t), 1.0)
                        if mm_i == 0:
                            w = w * (1.0 / math.sqrt(HEAD))
                        qkv[mm_i, ds(t), u * 128 : (u + 1) * 128] = w.astype(BF)
                return carry

            lax.fori_loop(0, NB, proj, 0)
        tick()
        gather_wait(NJ + 1)

        def gcx(t, carry):
            gctx[ds(t), :] = mm(gs[ds(t), :], wo[...], NT).astype(BF)
            return carry

        lax.fori_loop(0, NB, gcx, 0)
        tick()

        low_half = lax.broadcasted_iota(jnp.int32, (1, 128), 1) < HEAD

        for hp in range(CW // 128):
            lanes = pl.ds(hp * 128, 128)
            dkv[...] = jnp.zeros_like(dkv)
            for i in range(NB):
                rows = pl.ds(i * TT, TT)
                n = (i + 1) * TT
                qb = qkv[0, rows, lanes]
                gb = gctx[rows, lanes]
                kb = qkv[1, pl.ds(0, n), lanes]
                vb = qkv[2, pl.ds(0, n), lanes]
                res = []
                for hd in range(2):
                    mask = low_half if hd == 0 else jnp.logical_not(low_half)
                    zero = jnp.zeros_like(qb)
                    s = mm(jnp.where(mask, qb, zero), kb, NT)
                    ahead = lax.broadcasted_iota(jnp.int32, (TT, n), 1) - lax.broadcasted_iota(
                        jnp.int32, (TT, n), 0
                    )
                    s = jnp.where(ahead <= i * TT, s, -1e30)
                    p = jnp.exp(s - jnp.max(s, -1, keepdims=True))
                    p = p * (1.0 / jnp.sum(p, -1, keepdims=True))
                    pb = p.astype(BF)
                    dp = mm(jnp.where(mask, gb, zero), vb, NT)
                    dsc = (p * (dp - jnp.sum(p * dp, -1, keepdims=True))).astype(BF)
                    res.append(
                        (mm(pb, vb), mm(dsc, kb), mm(dsc, qb, TN), mm(pb, gb, TN))
                    )
                both = [jnp.where(low_half, u, w) for u, w in zip(res[0], res[1])]
                ctx[rows, lanes] = both[0].astype(BF)
                dq = turned(both[1] * (1.0 / math.sqrt(HEAD)), rows, -1.0)
                gproj[rows, pl.ds(hp * 128, 128)] = dq.astype(BF)
                dkv[0, pl.ds(0, n), :] += both[2]
                dkv[1, pl.ds(0, n), :] += both[3]
            for i in range(NB):
                rows = pl.ds(i * TT, TT)
                gproj[rows, pl.ds(CW + hp * 128, 128)] = turned(dkv[0, rows, :], rows, -1.0).astype(
                    BF
                )
                gproj[rows, pl.ds(2 * CW + hp * 128, 128)] = dkv[1, rows, :].astype(BF)
            tick()

        grad_piece(2 * NJ, gst_t, lambda: ctx[...], gst)
        for mm_i in range(3):
            grad_piece(
                2 * NJ + 1 + mm_i, n1t, lambda: gproj[:, mm_i * CW : (mm_i + 1) * CW], gst
            )
        tick()

        def att_out(s, carry):
            n1[ds(s), :] = mm(in_slot(ctx, s, CW), wo[...]).astype(BF)
            return carry

        lax.fori_loop(0, NB, att_out, 0)

        def hand(a, buf):
            @pl.when(c != y)
            def _():
                rcopy(buf, ar.at[a], s_ar[a], r_ar[a], fsdp=fs)

        hand(0, n1)

        def att_in(s, carry):
            e = mm(in_slot(gproj, s, 3 * CW), wqkv[...], NT)
            src, row = place(s)
            gs[ds(s), :] = norm_back(e, X3[src, row, :], vec(0), 0).astype(BF)
            return carry

        lax.fori_loop(0, NB, att_in, 0)
        hand(1, gs)

        for mm_i in range(3):
            gb = jnp.sum(gproj[:, mm_i * CW : (mm_i + 1) * CW].astype(F32), 0, keepdims=True)
            for xx in range(X):
                for cc in range(2):
                    nb = 2 * X * mm_i + 2 * xx + cc
                    at = nb // 3

                    @pl.when(c == cc)
                    def _():
                        sgv[9 + nb % 3 : 10 + nb % 3, at * RS : (at + 1) * RS] = gb[
                            :, xx * SW : (xx + 1) * SW
                        ]

        here = f * 2 + y
        lcopy(sgv, sgA.at[here], l_sga)
        for dev in near[: 4 * X - 1]:
            rcopy(sgv, sgA.at[here], s_sga, r_sga, **dev)
        tick()

        for a, buf in ((0, n1), (1, gs)):

            @pl.when(c == y)
            def _():
                wait(r_ar[a], ar.at[a])

                def take(s, carry):
                    lcopy(ar.at[a, ds(s)], stage, l_st).wait()
                    buf[ds(s), :] = (
                        buf[ds(s), :].astype(F32) + stage[...].astype(F32)
                    ).astype(BF)
                    return carry

                lax.fori_loop(0, NB, take, 0)
                rcopy(buf.at[ds(yo, R)], af.at[a], s_af[a], r_af[a], ctx=yo)
                lcopy(buf.at[ds(y, R)], af.at[a], l_af[a])

        tick()

        for a, buf in ((0, n1), (1, gs)):

            @pl.when(c == y)
            def _():
                wait(s_af[a], af.at[a])
                wait(l_af[a], af.at[a])

            @pl.when(c != y)
            def _():
                wait(s_ar[a], ar.at[a])
                wait(r_af[a], af.at[a])

        tick()

    s_sga, r_sga, l_sga = S(), S(), S()
    s_sgb, r_sgb, l_sgb = S(), S(), S()
    pl.run_scoped(
        attend,
        pltpu.VMEM((L, D), BF),
        pltpu.VMEM((D, L), BF),
        pltpu.VMEM((L, D), BF),
        pltpu.VMEM((D, L), BF),
        pltpu.VMEM((3, L, CW), BF),
        pltpu.VMEM((L, CW), BF),
        pltpu.VMEM((L, CW), BF),
        pltpu.VMEM((L, 3 * CW), BF),
        pltpu.VMEM((2, L, 128), F32),
        pltpu.VMEM((3, L, 128), F32),
        pltpu.VMEM((X, RX, CW), BF),
        pltpu.VMEM((TT, D), BF),
    )

    def finish(s1, s2, o1, o2):
        for a in range(2):
            wait(r_mo[a], mo.at[a])
        for i in range(R // TT):
            for a, dst, stg in ((0, out_ref, o1), (1, gin_ref, o2)):
                lcopy(mo.at[a, ds(i)], s1, l_st).wait()
                lcopy(af.at[a, ds(i)], s2, l_st).wait()
                total = tot[a, ds(i), :].astype(F32) + s1[...].astype(F32) + s2[...].astype(F32)
                stg[...] = total.astype(stg.dtype)
                lcopy(stg, dst.at[ds(i)], l_st).wait()

    wait(l_sga, sgv)
    wait(r_sga, sgA.at[pl.ds(0, 4 * X - 1)])
    total = sgA[0]
    for i in range(1, 4 * X):
        total = total + sgA[i]
    wait(s_sga, sgA.at[pl.ds(0, 4 * X - 1)])
    sgv[...] = total
    lcopy(sgv, sgB.at[r], l_sgb)
    for dev in near[4 * X - 1 :]:
        rcopy(sgv, sgB.at[r], s_sgb, r_sgb, **dev)

    pl.run_scoped(
        finish,
        pltpu.VMEM((TT, D), BF),
        pltpu.VMEM((TT, D), BF),
        pltpu.VMEM((TT, D), BF),
        pltpu.VMEM((TT, D), F32),
    )
    tick()
    wait(l_sgb, sgv)
    wait(r_sgb, sgB.at[pl.ds(0, NREP - 1)])
    wait(s_sgb, sgB.at[pl.ds(0, NREP - 1)])
    total = sgB[0]
    for i in range(1, NREP):
        total = total + sgB[i]
    sgv[...] = total
    lcopy(sgv, sg_ref, l_sga).wait()

    while live or waiting:
        tick()

    wait(s_sm, sm_v.at[pl.ds(0, 2 * X - 1)])
    wait(s_bo, oh_ref)
    for src, dst, ids in tok:
        wait(ids[1], src)
    for p in range(NP - SLOTS, NP):
        wait(ys[p], ysend.at[0])
    for fn in finals:
        fn()
    if h > 1:

        @pl.when(m > 0)
        def _():
            for p in range(NP):
                wait(zbs[p], own.at[0])


def sem_count(NJ, NREP):
    return 7 * (NJ + 2) + 11 * (2 * NJ + 4) + 64


def body(
    residual_in,
    block_order,
    ln1_gain,
    ln1_bias,
    ln2_gain,
    ln2_bias,
    w_qkv,
    b_qkv,
    w_out,
    b_out,
    w_up,
    b_up,
    w_down,
    b_down,
    cotangent,
):
    R, D = residual_in.shape[1:]
    FF = w_up.shape[1]
    NF = lax.axis_size("fsdp")
    NREP = lax.axis_size("rep")
    X = NF // 2
    L, RX, RS = 2 * R, D // X, D // NF
    NJ = FF // 2 // CW
    NP = 2 * NJ + 4
    f = lax.axis_index("fsdp")

    order = block_order[0]
    count = order.shape[0]
    spots = jnp.arange(count, dtype=jnp.int32)
    where = (order[None, :] == spots[:, None]).astype(F32).reshape(-1, 1)
    where = jnp.broadcast_to(where, (count * count, 128))
    small = jnp.concatenate(
        [
            v.astype(F32).reshape(-1, RS)
            for v in (ln1_gain, ln1_bias, ln2_gain, ln2_bias, b_qkv, b_out, b_up, b_down)
        ]
        + [jnp.zeros((3, RS), F32)],
        0,
    )
    halves = ROT // 2
    lane = jnp.arange(128, dtype=jnp.int32) % HEAD
    inv = 10000.0 ** (-(2.0 * (lane % halves).astype(F32)) / ROT)
    angles = jnp.arange(L, dtype=F32)[:, None] * inv[None, :]
    turning = (lane < ROT)[None, :]
    first = (lane < halves)[None, :]
    cosine, sine = jnp.cos(angles), jnp.sin(angles)
    tab = jnp.stack(
        [
            jnp.where(turning, cosine, 1.0),
            jnp.where(turning & ~first, sine, 0.0),
            jnp.where(first, -sine, 0.0),
        ]
    )

    anywhere = pl.BlockSpec(memory_space=pl.ANY)
    sds = jax.ShapeDtypeStruct
    outs = pl.pallas_call(
        functools.partial(kernel, (X, NREP, R, D, FF)),
        out_shape=(
            sds((RS, FF), BF),
            sds((D, FF // NF), BF),
            sds((RS, 3 * D), BF),
            sds((D, RS), BF),
            sds((R, D), BF),
            sds((R, D), F32),
            sds((16, D), F32),
            sds((NP, X, RX, CW), BF),
            sds((NP, X - 1, RX, CW), BF),
            sds((2, L, D), BF),
            sds((2, R, D), BF),
            sds((2, R, D), BF),
        ),
        in_specs=[anywhere] * 9,
        out_specs=(anywhere,) * 12,
        scratch_shapes=[
            pltpu.VMEM((3, R, D), BF),
            pltpu.VMEM((3, R, D), BF),
            pltpu.VMEM((NJ, D, CW), BF),
            pltpu.VMEM((NJ, CW, D), BF),
            pltpu.VMEM((D, 3 * CW), BF),
            pltpu.VMEM((CW, D), BF),
            pltpu.VMEM((2, (L // TT) ** 2, 128), F32),
            pltpu.VMEM((NF, 16, RS), F32),
            pltpu.VMEM((16, D), F32),
            pltpu.VMEM((16, D), F32),
            pltpu.VMEM((2 * NF, 16, D), F32),
            pltpu.VMEM((NREP, 16, D), F32),
            pltpu.VMEM((NP, RX, HW), BF),
            pltpu.VMEM((NP, RX, HW), BF),
            pltpu.VMEM((NP, RX, HW), BF),
            pltpu.VMEM((NP, RX, HW), BF),
            pltpu.VMEM((SLOTS, RX, HW), BF),
            pltpu.VMEM((2 * X, RX, HW), BF),
            pltpu.VMEM((2, R, D), BF),
            pltpu.SemaphoreType.DMA((sem_count(NJ, NREP),)),
        ],
        compiler_params=pltpu.CompilerParams(
            collective_id=0, has_side_effects=True, vmem_limit_bytes=63 * 1024 * 1024
        ),
    )(
        residual_in.reshape(R, D),
        cotangent.reshape(R, D),
        where,
        small,
        w_qkv,
        w_out,
        w_up,
        w_down,
        tab,
    )
    fin_up, fin_dn, fin_qkv, fin_o, out, gin, sg = outs[:7]
    mine = lax.dynamic_slice(sg, (0, f * RS), (16, RS))
    return (
        out[None],
        gin[None],
        mine[0],
        mine[1],
        mine[2],
        mine[3],
        fin_qkv.astype(F32),
        mine[9:12].reshape(-1),
        fin_o.astype(F32).T,
        mine[4],
        fin_up.astype(F32),
        mine[5:9].reshape(-1),
        fin_dn.astype(F32).T,
        mine[4],
    )


def solution(mesh):
    in_specs = (
        P(("rep", "fsdp"), "ctx", None),
        P(("rep", "fsdp"), None),
        P("fsdp"),
        P("fsdp"),
        P("fsdp"),
        P("fsdp"),
        P("fsdp", None),
        P("fsdp"),
        P("fsdp", None),
        P("fsdp"),
        P("fsdp", None),
        P("fsdp"),
        P("fsdp", None),
        P("fsdp"),
        P(("rep", "fsdp"), "ctx", None),
    )
    out_specs = (
        P(("rep", "fsdp"), "ctx", None),
        P(("rep", "fsdp"), "ctx", None),
        P("fsdp"),
        P("fsdp"),
        P("fsdp"),
        P("fsdp"),
        P("fsdp", None),
        P("fsdp"),
        P("fsdp", None),
        P("fsdp"),
        P("fsdp", None),
        P("fsdp"),
        P("fsdp", None),
        P("fsdp"),
    )
    return jax.shard_map(body, mesh=mesh, in_specs=in_specs, out_specs=out_specs, check_vma=False)
```

time: 1390 us -> 346 us (0.25)
  waiting for transfers between devices: 934 us -> 0 us
  Pallas kernels: 0 us -> 311 us
  matrix products: 195 us -> 0 us
  blocking collectives: 93.2 us -> 0 us
  local copies, waits for them, and re-layouts: 68.2 us -> 17.3 us
  other arithmetic: 56.8 us -> 12 us
  loops' own time: 21.7 us -> 0 us
  between operations: 16.7 us -> 1.1 us
    reduce_scatter x6 -> x0, waiting for transfers between devices: 469 us -> none  [the longest x1 129 us: body(): lax.psum_scatter(grads[8], 'fsdp', scatter_dimension=0, tiled=True)]
    psum x1 -> x0, waiting for transfers between devices: 313 us -> none  [body(): lax.psum((shards[0], shards[1], shards[2], shards[3], shards[4], shards[5...]
    pallas_call x0 -> x1, Pallas kernels: none -> 311 us  [body(): pl.pallas_call(functools.partial(kernel, (X, NREP, R, D, FF)), out_shape=...]
    dot_general x40 -> x0, matrix products: 195 us -> none  [the longest x8 31.5 us: masked_scores(): jnp.einsum('qgd,kgd->gqk', query_blk, key_blk, preferred_element_type=jnp...]
    all_gather x6 -> x0, waiting for transfers between devices: 149 us -> none  [the longest x1 32.3 us: body(): lax.all_gather(w_down, 'fsdp', axis=0, tiled=True)]
    all_gather x8 -> x0, blocking collectives: 41.9 us -> none  [the longest x1 6.14 us: body(): lax.all_gather(b_qkv, 'fsdp', axis=0, tiled=True)]
    psum x1 -> x0, blocking collectives: 39.7 us -> none  [body(): lax.psum((shards[0], shards[1], shards[2], shards[3], shards[4], shards[5...]
    dynamic_slice x32 -> x0, local copies, waits for them, and re-layouts: 26.3 us -> none  [the longest x24 21.2 us: slab_of(): lax.dynamic_slice(array, (seq_idx, row_start, column), (1, length, column...]
  transfers between devices with their start and end apart: 13 -> 0, of which waited for: 12 -> 0; matrix products, arithmetic and copies ran while one was open for 11% -> 0% of each run, Pallas kernels for 0% -> 0%
where the time goes in v1:
time: 346 us; the launch traced here: 341 us
  Pallas kernels  311 us (90%)
  local copies, waits for them, and re-layouts  17.3 us (5%)
  other arithmetic  12 us (3%)
    pallas_call x1, Pallas kernels, body(): pl.pallas_call(functools.partial(kernel, (X, NREP, R, D, FF)), out_shape=...  311 us
    unnamed x35, local copies, waits for them, and re-layouts  12.4 us

profile of v1, /device:TPU:0, one launch (start us, length us, event | category | flops | bytes accessed | tf_op | source)
XLA Modules:
  0.0 341.4 jit_solution(8773524387532323217)
XLA Ops:
  0.7 0.0 copy-start.5
  0.7 0.0 copy-start.6
  0.7 0.0 copy-start.8
  0.7 0.0 copy-start.9
  0.7 0.0 copy-start.10
  0.7 0.0 copy-start.11
  0.8 0.0 copy-start.12
  0.8 0.0 copy-start.13
  0.8 0.0 copy-start.7
  0.8 2.0 cosine_select_fusion
  2.8 1.2 pad_maximum_fusion.tab_ref
  4.1 0.0 copy-done.5
  4.1 0.0 copy-done.6
  4.1 0.0 copy-done.8
  4.1 0.0 copy-done.9
  4.1 0.0 copy-done.10
  4.1 0.0 copy-done.11
  4.2 0.0 copy-done.12
  4.2 0.0 copy-done.13
  4.2 1.2 concatenate.3.sm_ref
  5.4 0.0 copy-done.7
  5.5 0.1 reshape.322
  5.5 0.7 broadcast_in_dim.45.oh_ref
  6.2 311.0 %shard_map.254 = (bf16[256,4096]{1,0:T(8,128)(2,1)}, bf16[1024,1024]{1,0:T(8,128)(2,1)}, bf16[256,3072]{1,0:T(8,128)(2,1)}, bf16[1024,256]{1,0:T(8,128)(2,1)}, b...) custom-call(bf16[512,1024]{1,0:T(8,128)(2,1)} %bitcast.25, ...), custom_call_target="tpu_custom_call" | custom-call | tf_op jit(solution)/shard_map/pallas_call | solution.py:963
  317.2 1.5 fusion.9
  318.7 0.0 copy-start.4
  318.7 0.8 dynamic-slice_bitcast_fusion
  319.5 0.6 copy.31
  320.1 0.8 dynamic-slice.4
  320.9 0.6 reshape.320
  321.5 4.1 %convert_bitcast_fusion = f32[1024,1024]{0,1:T(8,128)} fusion(bf16[1024,1024]{1,0:T(8,128)(2,1)} %get-tuple-element.27), kind=kLoop, calls=%fused_computation | loop fusion | flops 1048576 | bytes 6291456 | tf_op jit(solution)/shard_map/transpose | solution.py:1032
  325.6 0.0 copy-start
  325.6 5.5 %copy.30 = f32[1024,1024]{1,0:T(8,128)} copy(f32[1024,1024]{0,1:T(8,128)} %convert_bitcast_fusion) | data formatting | bytes 8388608
  331.1 0.0 copy-done
  331.1 0.0 copy-start.2
  331.1 2.5 convert_element_type.41
  333.6 0.0 copy-done.2
  333.6 0.0 copy-start.3
  333.6 2.0 convert_element_type.40
  335.6 0.0 copy-done.3
  335.6 0.1 convert_bitcast_fusion.1
  335.7 0.0 copy-start.1
  335.7 1.3 copy.29
  337.0 0.0 copy-done.4
  337.0 0.6 copy.35
  337.6 2.3 copy.36
  339.8 0.0 copy-done.1
  339.8 1.3 copy.37
  (13 shorter events, 0.1 us)
Async XLA Ops:
  0.7 3.4 copy-start.5
  0.7 3.4 copy-start.6
  0.7 3.4 copy-start.8
  0.7 3.4 copy-start.9
  0.7 3.4 copy-start.10
  0.7 3.4 copy-start.11
  0.8 3.4 copy-start.12
  0.8 3.4 %copy-start.13 = (bf16[256]{0:T(256)(128)(2,1)S(1)}, bf16[256]{0:T(256)(128)(2,1)}, u32[]{:S(2)}) copy-start(bf16[256]{0:T(256)(128)(2,1)} %param.28) | copy-start | bytes 1540
  0.8 4.7 %copy-start.7 = (s32[1,4]{1,0:T(1,128)S(1)}, s32[1,4]{1,0:T(1,128)}, u32[]{:S(2)}) copy-start(s32[1,4]{1,0:T(1,128)} %param.16) | copy-start | bytes 52
  318.7 18.3 %copy-start.4 = (f32[1,256]{1,0:T(1,128)}, f32[1,256]{1,0:T(1,128)S(1)}, u32[]{:S(2)}) copy-start(f32[1,256]{1,0:T(1,128)S(1)} %get-tuple-element.42) | copy-start | bytes 3076
  325.6 5.5 %copy-start = (bf16[256,4096]{1,0:T(8,128)(2,1)S(1)}, bf16[256,4096]{1,0:T(8,128)(2,1)}, u32[]{:S(2)}) copy-start(bf16[256,4096]{1,0:T(8,128)(2,1)} %get-tuple-element.26) | copy-start | bytes 6291460
  331.1 2.5 copy-start.2
  333.6 2.0 copy-start.3
  335.7 4.1 %copy-start.1 = (f32[512,1024]{1,0:T(8,128)S(1)}, f32[512,1024]{1,0:T(8,128)}, u32[]{:S(2)}) copy-start(f32[512,1024]{1,0:T(8,128)} %get-tuple-element.22) | copy-start | bytes 6291460

commit v2 on v1

v2 whole, which is shorter than its diff:
```python
import functools
import math

import jax
import jax.numpy as jnp
import numpy as np
from jax import lax
from jax.experimental import pallas as pl
from jax.experimental.pallas import tpu as pltpu
from jax.sharding import PartitionSpec as P

HEADS = 16
HEAD = 64
ROT = 16
BLK = 256
EPSILON = 1e-05
PW = 256
TT = 256
FLIGHT = 4
LINK = pl.DeviceIdType.MESH
BF = jnp.bfloat16
F32 = jnp.float32

NN = (((1,), (0,)), ((), ()))
NT = (((1,), (1,)), ((), ()))
TN = (((0,), (0,)), ((), ()))


def mm(a, b, dims=NN):
    return lax.dot_general(a, b, dims, preferred_element_type=F32)


def mult(value, of):
    return value if isinstance(value, int) else pl.multiple_of(value, of)


def kernel(
    dims,
    x_ref,
    g_ref,
    oh_ref,
    sm_ref,
    wqkv_ref,
    wo_ref,
    wup_ref,
    wdn_ref,
    tab_ref,
    fin_up,
    fin_dn,
    fin_qkv,
    fin_o,
    out_ref,
    gin_ref,
    sg_ref,
    gbuf,
    mo,
    af,
    X4,
    G4,
    wup,
    wdn,
    wqkv,
    wo,
    oh_v,
    sm_v,
    vecs,
    sgv,
    sgA,
    sgB,
    own,
    zin,
    zback,
    xrecv,
    OB,
    TB,
    sems,
):
    X, NREP, R, D, FF = dims
    L = 2 * R
    T = 2 * L
    RX = D // X
    RS = D // (2 * X)
    FL = FF // 4
    HC = D // 4
    FX, HX = FL // X, HC // X
    NB = L // TT
    NU = FL // PW
    NP = 2 * NU + 4

    f = lax.axis_index("fsdp")
    y = lax.axis_index("ctx")
    r = lax.axis_index("rep")
    c = lax.rem(f, 2)
    xi = lax.div(f, 2)
    fs = xi * 2 + (1 - c)
    yo = 1 - y

    counter = [0]

    def S():
        counter[0] += 1
        return counter[0] - 1

    def rcopy(src, dst, ss, rs, **dev):
        cp = pltpu.make_async_remote_copy(
            src_ref=src,
            dst_ref=dst,
            send_sem=sems.at[ss],
            recv_sem=sems.at[rs],
            device_id=dev,
            device_id_type=LINK,
        )
        cp.start()
        return cp

    def lcopy(src, dst, s):
        cp = pltpu.make_async_copy(src, dst, sems.at[s])
        cp.start()
        return cp

    def wait(s, ref):
        pltpu.make_async_copy(ref, ref, sems.at[s]).wait()

    def ds(i, size=TT):
        return pl.ds(mult(i * size, size), size)

    finals = []

    NG = 4
    gxs = [S() for _ in range(NG)]
    gxr = [S() for _ in range(NG)]
    gzs = [S() for _ in range(NG)]
    gzr = [S() for _ in range(NG)]
    gcs = [S() for _ in range(NG)]
    gcr = [S() for _ in range(NG)]
    gl = [S() for _ in range(NG)]
    q = lax.rem(r, 2)
    zp = r + 1 - 2 * q
    dest = [wup, wdn, wqkv, wo]

    def cols(k, ct):
        if k == 0:
            for xx in range(X):
                at = (FF // X) * xx + (FF // (2 * X)) * ct + FX * y
                yield wup_ref, mult(at, 128), xx * FX, FX
        elif HX >= 128:
            for m in range(3):
                for xx in range(X):
                    at = D * m + (D // X) * xx + (D // (2 * X)) * ct + HX * y
                    yield wqkv_ref, mult(at, 128), m * HC + xx * HX, HX
        else:
            yield wqkv_ref, mult((2 * ct + y) * 3 * HC, 128), 0, 3 * HC

    def part(ref, row, n, col, w):
        return ref.at[pl.ds(row, n), pl.ds(col, w)]

    def span(ref, row, n):
        return ref.at[pl.ds(row, n)]

    def xz_bytes(k):
        if k < 2:
            return gbuf.at[pl.ds(0, 2), pl.ds(0, X - 1)]
        return gbuf.at[pl.ds(0, 3 if k == 2 else 1), pl.ds(0, X - 1), pl.ds(0, RX // 2)]

    def core_bytes(k):
        if k == 0:
            return gbuf.at[pl.ds(0, 2), 0]
        return gbuf.at[pl.ds(0, 3), 0, pl.ds(0, RX // 2)]

    def local_bytes(k):
        if k == 2:
            return core_bytes(k)
        return gbuf.at[pl.ds(0, (2, 4, 0, 1)[k]), 0]

    def rows_of(k):
        return (wdn_ref, FX) if k == 1 else (wo_ref, HX)

    def gather_x(k):
        for dx in range(1, X):
            xo = lax.rem(xi + dx, X)
            if k in (0, 2):
                n = RS // 2
                r0 = mult(q * n, n)
                for ct in range(2):
                    for src, sc, dc, w in cols(k, ct):
                        rcopy(
                            part(src, r0, n, sc, w),
                            part(dest[k], mult(RS * f + r0, n), n, dc, w),
                            gxs[k],
                            gxr[k],
                            fsdp=2 * xo + ct,
                        )
            else:
                src, w = rows_of(k)
                n = w // 2
                rcopy(
                    span(src, mult(w * y + q * n, n), n),
                    span(dest[k], mult(w * xi + q * n, n), n),
                    gxs[k],
                    gxr[k],
                    fsdp=2 * xo + c,
                )
        finals.append(lambda: wait(gxs[k], xz_bytes(k)))

    def gather_fwd(k):
        wait(gxr[k], xz_bytes(k))
        for dx in range(1, X):
            xo = lax.rem(xi + dx, X)
            if k in (0, 2):
                n = RS // 2
                for ct in range(2):
                    piece = span(dest[k], mult(RS * (2 * xo + ct) + q * n, n), n)
                    rcopy(piece, piece, gzs[k], gzr[k], rep=zp)
            else:
                _, w = rows_of(k)
                piece = span(dest[k], mult(w * xo + q * (w // 2), w // 2), w // 2)
                rcopy(piece, piece, gzs[k], gzr[k], rep=zp)
        if k > 1:
            finals.append(lambda: wait(gzs[k], xz_bytes(k)))

    def gather_core(k):
        if k in (0, 2):
            rows = mult(RS * f, RS)
            for src, sc, dc, w in cols(k, 1 - c):
                rcopy(
                    part(src, 0, RS, sc, w), part(dest[k], rows, RS, dc, w), gcs[k], gcr[k], fsdp=fs
                )
            for src, sc, dc, w in cols(k, c):
                lcopy(part(src, 0, RS, sc, w), part(dest[k], rows, RS, dc, w), gl[k])
            finals.append(lambda: wait(gcs[k], core_bytes(k)))
        else:
            src, w = rows_of(k)
            lcopy(span(src, mult(w * y, w), w), span(dest[k], mult(w * xi, w), w), gl[k])

    def gather_wait(k):
        wait(gl[k], local_bytes(k))
        if k in (0, 2):
            wait(gcr[k], core_bytes(k))
        wait(gzr[k], xz_bytes(k))

    xs = [S() for _ in range(NP)]
    xr = [S() for _ in range(NP)]
    zis = [S() for _ in range(NP)]
    zir = [S() for _ in range(NP)]
    zbs = [S() for _ in range(NP)]
    zbr = [S() for _ in range(NP)]
    ags = [S() for _ in range(NP)]
    agr = [S() for _ in range(NP)]
    agl = [S() for _ in range(NP)]
    lp = [S() for _ in range(2)]
    held = []

    h = NREP // 2
    depth = jnp.where(r < h, r, NREP - 1 - r)
    inner = jnp.where(r < h, r + 1, r - 1)
    outer = jnp.where(r < h, r - 1, r + 1)

    def is_up(p):
        return p < NU or p > 2 * NU

    def x_bytes():
        return gbuf.at[0, pl.ds(0, X - 1)]

    def send_x(p):
        for dx in range(1, X):
            xo = lax.rem(xi + dx, X)
            rcopy(gbuf.at[p, xo], xrecv.at[p, dx - 1], xs[p], xr[p], fsdp=2 * xo + c)
        finals.append(lambda: wait(xs[p], x_bytes()))

    def add_rows(count, fn):
        def step(i, carry):
            fn(ds(i, 64))
            return carry

        lax.fori_loop(0, count // 64, step, 0)

    def add_into(p, dst, other):
        def add(rows):
            dst[p, rows, :] = (own[p, rows, :].astype(F32) + other[p, rows, :].astype(F32)).astype(
                BF
            )

        add_rows(RX, add)

    def send_in(p, at_middle):
        if at_middle:
            rcopy(own.at[p], zback.at[p], zis[p], zbr[p], rep=inner)
        else:
            rcopy(own.at[p], zin.at[p], zis[p], zir[p], rep=inner)

    def stage_x(p):
        wait(xr[p], x_bytes())

        def add(rows):
            total = own[p, rows, :].astype(F32)
            for d in range(X - 1):
                total = total + xrecv[p, d, rows, :].astype(F32)
            own[p, rows, :] = total.astype(BF)

        add_rows(RX, add)

        @pl.when(depth == 0)
        def _():
            send_in(p, h == 1)

        finals.append(lambda: wait(zis[p], own.at[0]))

    def stage_in(k, p):
        @pl.when(depth == k)
        def _():
            wait(zir[p], own.at[0])
            add_into(p, own, zin)
            send_in(p, k == h - 1)

    def stage_out(i, p):
        @pl.when(depth == h - 1 - i)
        def _():
            wait(zbr[p], own.at[0])
            if i == 0:
                add_into(p, zback, zback)
            if h - 1 - i > 0:
                rcopy(zback.at[p], zback.at[p], zbs[p], zbr[p], rep=outer)

    def ag_bytes(p):
        return own.at[pl.ds(0, 3), pl.ds(0, RS)] if is_up(p) else own.at[0]

    def up_places(p):
        if p < NU:
            xx, off = p * PW // FX, p * PW % FX
            at = (FF // X) * xx + (FF // (2 * X)) * c + FX * y + off
            return [(0, PW, fin_up, mult(at, 128))]
        m = p - 2 * NU - 1
        if HX >= 128:
            return [
                (xx * HX, HX, fin_qkv, mult(D * m + (D // X) * xx + (D // (2 * X)) * c + HX * y, 128))
                for xx in range(X)
            ]
        return [(0, HC, fin_qkv, mult((2 * c + y) * 3 * HC + m * HC, 128))]

    def stage_ag(p):
        if is_up(p):
            for lane, w, dst, at in up_places(p):
                mine = zback.at[p, ds(c, RS), pl.ds(lane, w)]
                theirs = zback.at[p, ds(1 - c, RS), pl.ds(lane, w)]
                to = dst.at[:, pl.ds(at, w)]
                rcopy(mine, to, ags[p], agr[p], ctx=yo)
                rcopy(theirs, to, ags[p], agr[p], fsdp=fs, ctx=yo)
                rcopy(theirs, to, ags[p], agr[p], fsdp=fs)
                lcopy(mine, to, agl[p])
        else:
            if p < 2 * NU:
                pairs = [(zback.at[p], fin_dn.at[ds(y, RX), pl.ds((p - NU) * PW, PW)])]
            else:
                pairs = [
                    (
                        zback.at[p, pl.ds(b * HX, HX)],
                        fin_o.at[pl.ds(mult(y * HX, HX), HX), pl.ds(b * PW, PW)],
                    )
                    for b in range(RX // HX)
                ]
            for src, to in pairs:
                rcopy(src, to, ags[p], agr[p], ctx=yo)
                lcopy(src, to, agl[p])
        finals.append(lambda: wait(agl[p], own.at[0, pl.ds(0, RS)] if is_up(p) else own.at[0]))
        finals.append(lambda: wait(ags[p], ag_bytes(p)))
        finals.append(lambda: wait(agr[p], ag_bytes(p)))

    stages = [stage_x]
    for k in range(1, h):
        stages.append(functools.partial(stage_in, k))
    for i in range(h - 1):
        stages.append(functools.partial(stage_out, i))

    def stage_last(p):
        stage_out(h - 1, p)
        stage_ag(p)

    stages.append(stage_last)
    lag = [1] * len(stages)
    live = []
    moving = []
    ready = []
    clock = [0]

    def push():
        while ready and len(moving) < FLIGHT:
            send_x(ready[0])
            moving.append(ready.pop(0))

    def tick(count=1, drain=False):
        clock[0] += 1
        fresh = []
        for item in list(live):
            p, s, due = item
            if drain or clock[0] >= due:
                stages[s](p)
                if s == len(stages) - 1:
                    live.remove(item)
                else:
                    item[1:] = [s + 1, clock[0] + lag[s]]
        for _ in range(count):
            if moving:
                p = moving.pop(0)
                stages[0](p)
                push()
                fresh.append([p, 1, clock[0] + lag[0]])
        live.extend(fresh)

    def flush():
        while held:
            p, gst = held.pop(0)
            wait(lp[p % 2], gst)
            ready.append(p)
        push()

    def grad_piece(p, lhs_t, rhs, both):
        gst = both.at[p % 2]
        if is_up(p) or p < 2 * NU:

            def step(t, carry):
                gst[t] = mm(lhs_t[ds(t, RX), :], rhs()).astype(BF)
                return carry

            lax.fori_loop(0, X, step, 0)
        else:
            res = mm(lhs_t[...], rhs()).astype(BF)
            for xx in range(X):
                for b in range(RX // HX):
                    gst[xx, b * HX : (b + 1) * HX, :] = res[
                        xx * HX : (xx + 1) * HX, b * PW : (b + 1) * PW
                    ]
        own[p] = gst[xi]
        flush()
        lcopy(gst, gbuf.at[p], lp[p % 2])
        held.append((p, gst))

    bar = pltpu.get_barrier_semaphore()
    near = []
    for df in range(2 * X):
        for dy in range(2):
            if df or dy:
                near.append(dict(fsdp=lax.rem(f + df, 2 * X), ctx=lax.rem(y + dy, 2)))
    for dr in range(1, NREP):
        near.append(dict(rep=lax.rem(r + dr, NREP)))
    for dev in near:
        pl.semaphore_signal(bar, inc=1, device_id=dev, device_id_type=LINK)
    pl.semaphore_wait(bar, len(near))

    gather_x(0)
    tok = []
    home = ds(2 * c + y, R)
    for src, dst in ((x_ref, X4), (g_ref, G4)):
        ids = [S() for _ in range(7)]
        lcopy(src, dst.at[home], ids[0])
        rcopy(src, dst.at[home], ids[1], ids[2], fsdp=fs)
        rcopy(src, dst.at[home], ids[3], ids[4], ctx=yo)
        tok.append((src, dst, ids))
    s_sm, r_sm, l_sm = S(), S(), S()
    lcopy(sm_ref, sm_v.at[f], l_sm)
    for df in range(1, 2 * X):
        rcopy(sm_ref, sm_v.at[f], s_sm, r_sm, fsdp=lax.rem(f + df, 2 * X))
    s_oh, r_oh, l_oh = S(), S(), S()
    lcopy(oh_ref, oh_v.at[c], l_oh)
    rcopy(oh_ref, oh_v.at[c], s_oh, r_oh, fsdp=fs)
    for k in range(NG):
        gather_core(k)

    def exchange_forward():
        for src, dst, ids in tok:
            piece = dst.at[ds(2 * c + yo, R)]
            wait(ids[4], src)
            rcopy(piece, piece, ids[5], ids[6], fsdp=fs)

    def exchange_finish():
        for src, dst, ids in tok:
            wait(ids[6], src)

    wait(l_sm, sm_ref)
    wait(r_sm, sm_v.at[pl.ds(0, 2 * X - 1)])
    for ff in range(2 * X):
        vecs[:, ff * RS : (ff + 1) * RS] = sm_v[ff]
    sgv[...] = jnp.zeros_like(sgv)
    for src, dst, ids in tok:
        wait(ids[0], src)
        wait(ids[2], src)

    def vec(row):
        return vecs[row : row + 1, :]

    def center(blk):
        v = blk.astype(F32)
        mid = v - jnp.mean(v, -1, keepdims=True)
        rs = lax.rsqrt(jnp.mean(mid * mid, -1, keepdims=True) + EPSILON)
        return mid * rs, rs

    def norm_back(e, n, rs, gain, row):
        sgv[row : row + 1, :] += jnp.sum(e * n, 0, keepdims=True)
        sgv[row + 1 : row + 2, :] += jnp.sum(e, 0, keepdims=True)
        eg = e * gain
        return rs * (
            eg - jnp.mean(eg, -1, keepdims=True) - n * jnp.mean(eg * n, -1, keepdims=True)
        )

    def feed(n2t, hidt, gup, gst):
        def gsum(b, carry):
            at = pl.ds(mult((2 * c + y) * R + b * TT, TT), TT)
            sgv[4:5, :] += jnp.sum(G4[at, :].astype(F32), 0, keepdims=True)
            return carry

        lax.fori_loop(0, R // TT, gsum, 0)
        bias = jnp.concatenate(
            [
                jnp.where(
                    y == 0,
                    vecs[8 + rr : 9 + rr, ds(2 * xx + c, RS)],
                    vecs[10 + rr : 11 + rr, ds(2 * xx + c, RS)],
                )
                for xx in range(X)
                for rr in range(2)
            ],
            1,
        )
        gather_fwd(0)
        gather_x(1)
        gather_fwd(1)
        gather_x(2)
        gather_x(3)
        gather_wait(0)
        gather_wait(1)
        half_tiles = T // TT // 2

        def tile(i, gb):
            @pl.when(i == half_tiles - 1)
            def _():
                exchange_forward()

            @pl.when(i == half_tiles)
            def _():
                exchange_finish()

            yy = jnp.where(i < half_tiles, y, yo)
            j = lax.rem(i, half_tiles)
            per = R // TT
            rows = pl.ds(mult((2 * lax.div(j, per) + yy) * R + lax.rem(j, per) * TT, TT), TT)
            n, rs = center(X4[rows, :])
            n2 = (n * vec(2) + vec(3)).astype(BF)
            n2t[:, rows] = n2.T
            up = mm(n2, wup[...]) + bias
            cdf = 0.5 + 0.5 * lax.erf(up * (1.0 / math.sqrt(2.0)))
            hd = (up * cdf).astype(BF)
            hidt[:, rows] = hd.T
            gh = mm(G4[rows, :], wdn[...], NT)
            pdf = jnp.exp(-0.5 * up * up) * (1.0 / math.sqrt(2.0 * math.pi))
            gu = (gh * (cdf + up * pdf)).astype(BF)
            gup[rows, :] = gu
            OB[rows, :] = mm(hd, wdn[...]).astype(BF)
            gn = mm(gu, wup[...], NT)
            TB[rows, :] = norm_back(gn, n, rs, vec(2), 2).astype(BF)
            return gb + jnp.sum(gu.astype(F32), 0, keepdims=True)

        gb = lax.fori_loop(0, T // TT, tile, jnp.zeros((1, FL), F32))
        for yy in range(2):

            @pl.when(y == yy)
            def _():
                for xx in range(X):
                    for rr in range(2):
                        at = (2 * xx + rr) * RS
                        row = 5 + 2 * yy + rr
                        sgv[row : row + 1, ds(2 * xx + c, RS)] = gb[:, at : at + RS]

        gather_fwd(2)
        gather_fwd(3)
        for t in range(NU):
            grad_piece(t, n2t, lambda: gup[:, t * PW : (t + 1) * PW], gst)
        for t in range(NU):
            tick(1)
            grad_piece(NU + t, hidt, lambda: G4[:, t * PW : (t + 1) * PW], gst)
        flush()

    pl.run_scoped(
        feed,
        pltpu.VMEM((D, T), BF),
        pltpu.VMEM((FL, T), BF),
        pltpu.VMEM((T, FL), BF),
        pltpu.VMEM((2, X, RX, PW), BF),
    )

    s_mo = [S() for _ in range(2)]
    r_mo = [S() for _ in range(2)]
    s_af = [S() for _ in range(2)]
    r_af = [S() for _ in range(2)]
    l_tab, l_st, l_fin = S(), S(), S()
    s_sga, r_sga, l_sga = S(), S(), S()
    s_sgb, r_sgb, l_sgb = S(), S(), S()

    def give(a, buf):
        rcopy(buf.at[ds(1 - c, L)], mo.at[a], s_mo[a], r_mo[a], fsdp=fs)

    def take(a, buf, room):
        wait(r_mo[a], mo.at[a])
        wait(gzs[a], xz_bytes(a))
        lcopy(mo.at[a], room.at[pl.ds(0, L)], l_st).wait()

        def add(i, carry):
            rows = pl.ds(mult(c * L + i * 64, 64), 64)
            buf[rows, :] = (buf[rows, :].astype(F32) + room[ds(i, 64), :].astype(F32)).astype(BF)
            return carry

        lax.fori_loop(0, L // 64, add, 0)
        rcopy(buf.at[ds(2 * c + yo, R)], af.at[a], s_af[a], r_af[a], ctx=yo)

    def last(a, buf, room, dst):
        wait(r_af[a], af.at[a])
        lcopy(af.at[a], room.at[pl.ds(0, R)], l_st).wait()

        def add(i, carry):
            rows = pl.ds(mult((2 * c + y) * R + i * 64, 64), 64)
            total = buf[rows, :].astype(F32) + room[ds(i, 64), :].astype(F32)
            if a == 0:
                total = total + X4[rows, :].astype(F32) + vec(7) + vec(12)
            else:
                total = total + G4[rows, :].astype(F32)
            room[ds(i, 64), :] = total.astype(BF)
            return carry

        lax.fori_loop(0, R // 64, add, 0)
        lcopy(room.at[pl.ds(0, R)], dst, l_fin)

    def attend(n1t, ga, qkv, ctx, ctxt, gctx, gproj, dkv, tab, gst):
        lcopy(tab_ref, tab, l_tab)
        wait(l_oh, oh_ref)
        wait(r_oh, oh_ref)

        def weight(cc, b, s, width):
            w = oh_v[cc, pl.ds(b * NB + s, 1), :].astype(BF)
            return jnp.concatenate([w] * (width // 128), 1)

        def in_order(ref, cc, b):
            total = None
            for s in range(NB):
                rows = pl.ds(mult(cc * L + s * TT, TT), TT)
                term = ref[rows, :] * weight(cc, b, s, D)
                total = term if total is None else total + term
            return total

        def in_slot(ref, cc, s, width):
            total = None
            for b in range(NB):
                rows = pl.ds(mult(cc * L + b * TT, TT), TT)
                term = ref[rows, :] * weight(cc, b, s, width)
                total = term if total is None else total + term
            return total

        def turned(v, rows, sign):
            right = pltpu.roll(v, ROT // 2, 1)
            left = pltpu.roll(v, 128 - ROT // 2, 1)
            return v * tab[0, rows, :] + sign * (
                right * tab[1, rows, :] + left * tab[2, rows, :]
            )

        def pick(options):
            a = jnp.where(c == 0, options[0], options[2])
            b = jnp.where(c == 0, options[1], options[3])
            return jnp.where(y == 0, a, b)

        def spot(m, xx, cc, yy):
            e = D * m + (D // X) * xx + (D // (2 * X)) * cc + HX * yy
            rest = e % (3 * RS)
            return e // (3 * RS), rest // RS, rest % RS

        bias = jnp.concatenate(
            [
                pick(
                    [
                        jnp.concatenate(
                            [
                                sm_v[ff, 4 + row : 5 + row, lane : lane + HX]
                                for ff, row, lane in [spot(m, xx, cc, yy) for xx in range(X)]
                            ],
                            1,
                        )
                        for cc in range(2)
                        for yy in range(2)
                    ]
                )
                for m in range(3)
            ],
            1,
        )
        wait(l_tab, tab_ref)
        gather_wait(2)
        gather_wait(3)

        def prep(t, carry):
            cc, b = lax.div(t, NB), lax.rem(t, NB)
            n, _ = center(in_order(X4, cc, b))
            n1 = (n * vec(0) + vec(1)).astype(BF)
            n1t[:, ds(t)] = n1.T
            gv = in_order(G4, cc, b)
            ga[ds(t), :] = gv
            v = mm(n1, wqkv[...]) + bias
            for m in range(2):
                for u in range(HC // 128):
                    w = turned(v[:, m * HC + u * 128 : m * HC + (u + 1) * 128], ds(b), 1.0)
                    if m == 0:
                        w = w * (1.0 / math.sqrt(HEAD))
                    qkv[m, ds(t), u * 128 : (u + 1) * 128] = w.astype(BF)
            qkv[2, ds(t), :] = v[:, 2 * HC :].astype(BF)
            gctx[ds(t), :] = mm(gv, wo[...], NT).astype(BF)
            return carry

        lax.fori_loop(0, T // TT, prep, 0)
        tick(1)

        low_half = lax.broadcasted_iota(jnp.int32, (1, 128), 1) < HEAD
        dkv[...] = jnp.zeros_like(dkv)
        pairs = HC // 128
        for i in range(NB):
            n = (i + 1) * TT

            def pair(u, carry):
                cc, hp = lax.div(u, pairs), lax.rem(u, pairs)
                lanes = pl.ds(mult(hp * 128, 128), 128)
                rows = pl.ds(mult(cc * L + i * TT, TT), TT)
                seen = pl.ds(mult(cc * L, L), n)
                qb = qkv[0, rows, lanes]
                gb = gctx[rows, lanes]
                kb = qkv[1, seen, lanes]
                vb = qkv[2, seen, lanes]
                ahead = lax.broadcasted_iota(jnp.int32, (TT, n), 1) - lax.broadcasted_iota(
                    jnp.int32, (TT, n), 0
                )
                zero = jnp.zeros_like(qb)
                res = []
                for hd in range(2):
                    mask = low_half if hd == 0 else jnp.logical_not(low_half)
                    s = mm(jnp.where(mask, qb, zero), kb, NT)
                    s = jnp.where(ahead <= i * TT, s, -1e30)
                    p = jnp.exp(s - jnp.max(s, -1, keepdims=True))
                    p = p * (1.0 / jnp.sum(p, -1, keepdims=True))
                    pb = p.astype(BF)
                    dp = mm(jnp.where(mask, gb, zero), vb, NT)
                    dsc = (p * (dp - jnp.sum(p * dp, -1, keepdims=True))).astype(BF)
                    res.append((mm(pb, vb), mm(dsc, kb), mm(dsc, qb, TN), mm(pb, gb, TN)))
                both = [jnp.where(low_half, u0, u1) for u0, u1 in zip(res[0], res[1])]
                cb = both[0].astype(BF)
                ctx[rows, lanes] = cb
                ctxt[lanes, rows] = cb.T
                dq = turned(both[1] * (1.0 / math.sqrt(HEAD)), pl.ds(i * TT, TT), -1.0)
                gproj[rows, lanes] = dq.astype(BF)
                dkv[0, seen, lanes] += both[2]
                dkv[1, seen, lanes] += both[3]
                return carry

            lax.fori_loop(0, 2 * pairs, pair, 0)
            tick(1)

        def turn_back(t, carry):
            b = lax.rem(t, NB)
            for u in range(pairs):
                at = pl.ds(u * 128, 128)
                gproj[ds(t), HC + u * 128 : HC + (u + 1) * 128] = turned(
                    dkv[0, ds(t), at], ds(b), -1.0
                ).astype(BF)
            gproj[ds(t), 2 * HC : 3 * HC] = dkv[1, ds(t), :].astype(BF)
            return carry

        lax.fori_loop(0, T // TT, turn_back, 0)

        grad_piece(2 * NU, ctxt, lambda: ga[...], gst)
        for m in range(3):
            grad_piece(2 * NU + 1 + m, n1t, lambda: gproj[:, m * HC : (m + 1) * HC], gst)
        flush()

        def att_out(t, carry):
            cc, s = lax.div(t, NB), lax.rem(t, NB)
            a = mm(in_slot(ctx, cc, s, HC), wo[...])
            OB[ds(t), :] = (OB[ds(t), :].astype(F32) + a).astype(BF)
            return carry

        lax.fori_loop(0, T // TT, att_out, 0)
        give(0, OB)
        tick(1)

        def att_in(t, carry):
            cc, s = lax.div(t, NB), lax.rem(t, NB)
            e = mm(in_slot(gproj, cc, s, 3 * HC), wqkv[...], NT)
            n, rs = center(X4[ds(t), :])
            term = norm_back(e, n, rs, vec(0), 0)
            TB[ds(t), :] = (TB[ds(t), :].astype(F32) + term).astype(BF)
            return carry

        take(0, OB, wup)
        lax.fori_loop(0, T // TT, att_in, 0)
        give(1, TB)

        for m in range(3):
            gb = jnp.sum(gproj[:, m * HC : (m + 1) * HC].astype(F32), 0, keepdims=True)
            for cc in range(2):
                for yy in range(2):

                    @pl.when((c == cc) & (y == yy))
                    def _():
                        for xx in range(X):
                            ff, row, lane = spot(m, xx, cc, yy)
                            at = ff * RS + lane
                            sgv[9 + row : 10 + row, at : at + HX] = gb[:, xx * HX : (xx + 1) * HX]

    pl.run_scoped(
        attend,
        pltpu.VMEM((D, T), BF),
        pltpu.VMEM((T, D), BF),
        pltpu.VMEM((3, T, HC), BF),
        pltpu.VMEM((T, HC), BF),
        pltpu.VMEM((HC, T), BF),
        pltpu.VMEM((T, HC), BF),
        pltpu.VMEM((T, 3 * HC), BF),
        pltpu.VMEM((2, T, HC), F32),
        pltpu.VMEM((3, L, 128), F32),
        pltpu.VMEM((2, X, RX, PW), BF),
    )

    here = f * 2 + y
    lcopy(sgv, sgA.at[here], l_sga)
    for dev in near[: 4 * X - 1]:
        rcopy(sgv, sgA.at[here], s_sga, r_sga, **dev)
    tick(1)
    take(1, TB, wdn)
    wait(l_sga, sgv)
    wait(r_sga, sgA.at[pl.ds(0, 4 * X - 1)])
    total = sgA[0]
    for i in range(1, 4 * X):
        total = total + sgA[i]
    wait(s_sga, sgA.at[pl.ds(0, 4 * X - 1)])
    sgv[...] = total
    lcopy(sgv, sgB.at[r], l_sgb)
    for dev in near[4 * X - 1 :]:
        rcopy(sgv, sgB.at[r], s_sgb, r_sgb, **dev)
    tick(1)
    tick(1, True)
    tick(1, True)
    last(0, OB, wup, out_ref)
    wait(l_sgb, sgv)
    wait(r_sgb, sgB.at[pl.ds(0, NREP - 1)])
    wait(s_sgb, sgB.at[pl.ds(0, NREP - 1)])
    total = sgB[0]
    for i in range(1, NREP):
        total = total + sgB[i]
    sgv[...] = total
    lcopy(sgv, sg_ref, l_sga)
    while live or moving or ready:
        tick(1, True)
    last(1, TB, wdn, gin_ref)

    wait(l_sga, sgv)
    wait(l_fin, af)
    for a in range(2):
        wait(s_mo[a], mo.at[a])
        wait(s_af[a], af.at[a])
    wait(s_sm, sm_v.at[pl.ds(0, 2 * X - 1)])
    wait(s_oh, oh_ref)
    for src, dst, ids in tok:
        for k in (1, 3, 5):
            wait(ids[k], src)
    for fn in finals:
        fn()

    @pl.when(depth > 0)
    def _():
        for p in range(NP):
            wait(zbs[p], own.at[0])


def sem_count(NP):
    return 7 * 4 + 9 * NP + 64


def body(
    residual_in,
    block_order,
    ln1_gain,
    ln1_bias,
    ln2_gain,
    ln2_bias,
    w_qkv,
    b_qkv,
    w_out,
    b_out,
    w_up,
    b_up,
    w_down,
    b_down,
    cotangent,
):
    R, D = residual_in.shape[1:]
    FF = w_up.shape[1]
    NF = lax.axis_size("fsdp")
    NREP = lax.axis_size("rep")
    X = NF // 2
    L, T, RX, RS = 2 * R, 4 * R, D // X, D // NF
    FL, HC = FF // 4, D // 4
    HX = HC // X
    NP = 2 * (FL // PW) + 4
    f = lax.axis_index("fsdp")

    order = block_order[0]
    count = order.shape[0]
    spots = jnp.arange(count, dtype=jnp.int32)
    where = (order[None, :] == spots[:, None]).astype(F32).reshape(-1, 1)
    where = jnp.broadcast_to(where, (count * count, 128))
    small, at = None, 0
    for v in (ln1_gain, ln1_bias, ln2_gain, ln2_bias, b_qkv, b_out, b_up, b_down):
        n = v.shape[0]
        term = jnp.pad(v.astype(F32), (at, 16 * RS - at - n))
        small = term if small is None else small + term
        at += n
    small = small.reshape(16, RS)
    halves = ROT // 2
    lane = np.arange(128) % HEAD
    angles = np.arange(L)[:, None] * 10000.0 ** (-2.0 * (lane % halves) / ROT)[None, :]
    cosine, sine = np.cos(angles), np.sin(angles)
    tab = np.stack(
        [
            np.where(lane < ROT, cosine, 1.0),
            np.where((lane < ROT) & (lane >= halves), sine, 0.0),
            np.where(lane < halves, -sine, 0.0),
        ]
    ).astype(np.float32)

    def columns(w):
        if HX >= 128:
            return w
        w = w.reshape(RS, 3, X, 2, 2, HX).transpose(0, 3, 4, 1, 2, 5)
        return w.reshape(RS, 3 * D)

    def columns_back(w):
        if HX >= 128:
            return w
        w = w.reshape(RS, 2, 2, 3, X, HX).transpose(0, 3, 4, 1, 2, 5)
        return w.reshape(RS, 3 * D)

    anywhere = pl.BlockSpec(memory_space=pl.ANY)
    sds = jax.ShapeDtypeStruct
    outs = pl.pallas_call(
        functools.partial(kernel, (X, NREP, R, D, FF)),
        out_shape=(
            sds((RS, FF), BF),
            sds((FF // NF, D), BF),
            sds((RS, 3 * D), BF),
            sds((RS, D), BF),
            sds((R, D), BF),
            sds((R, D), BF),
            sds((16, D), F32),
            sds((NP, X, RX, PW), BF),
            sds((2, L, D), BF),
            sds((2, R, D), BF),
        ),
        in_specs=[anywhere] * 9,
        out_specs=(anywhere,) * 10,
        scratch_shapes=[
            pltpu.VMEM((T, D), BF),
            pltpu.VMEM((T, D), BF),
            pltpu.VMEM((D, FL), BF),
            pltpu.VMEM((FL, D), BF),
            pltpu.VMEM((D, 3 * HC), BF),
            pltpu.VMEM((HC, D), BF),
            pltpu.VMEM((2, (L // TT) ** 2, 128), F32),
            pltpu.VMEM((NF, 16, RS), F32),
            pltpu.VMEM((16, D), F32),
            pltpu.VMEM((16, D), F32),
            pltpu.VMEM((2 * NF, 16, D), F32),
            pltpu.VMEM((NREP, 16, D), F32),
            pltpu.VMEM((NP, RX, PW), BF),
            pltpu.VMEM((NP, RX, PW), BF),
            pltpu.VMEM((NP, RX, PW), BF),
            pltpu.VMEM((NP, X - 1, RX, PW), BF),
            pltpu.VMEM((T, D), BF),
            pltpu.VMEM((T, D), BF),
            pltpu.SemaphoreType.DMA((sem_count(NP),)),
        ],
        compiler_params=pltpu.CompilerParams(
            collective_id=0, has_side_effects=True, vmem_limit_bytes=63 * 1024 * 1024
        ),
    )(
        residual_in.reshape(R, D),
        cotangent.reshape(R, D),
        where,
        small,
        columns(w_qkv),
        w_out,
        w_up,
        w_down,
        tab,
    )
    fin_up, fin_dn, fin_qkv, fin_o, out, gin, sg = outs[:7]
    mine = lax.dynamic_slice(sg, (0, f * RS), (16, RS))
    return (
        out[None],
        gin.astype(F32)[None],
        mine[0],
        mine[1],
        mine[2],
        mine[3],
        columns_back(fin_qkv).astype(F32),
        mine[9:12].reshape(-1),
        fin_o.astype(F32),
        mine[4],
        fin_up.astype(F32),
        mine[5:9].reshape(-1),
        fin_dn.astype(F32),
        mine[4],
    )


def solution(mesh):
    in_specs = (
        P(("rep", "fsdp"), "ctx", None),
        P(("rep", "fsdp"), None),
        P("fsdp"),
        P("fsdp"),
        P("fsdp"),
        P("fsdp"),
        P("fsdp", None),
        P("fsdp"),
        P("fsdp", None),
        P("fsdp"),
        P("fsdp", None),
        P("fsdp"),
        P("fsdp", None),
        P("fsdp"),
        P(("rep", "fsdp"), "ctx", None),
    )
    out_specs = (
        P(("rep", "fsdp"), "ctx", None),
        P(("rep", "fsdp"), "ctx", None),
        P("fsdp"),
        P("fsdp"),
        P("fsdp"),
        P("fsdp"),
        P("fsdp", None),
        P("fsdp"),
        P("fsdp", None),
        P("fsdp"),
        P("fsdp", None),
        P("fsdp"),
        P("fsdp", None),
        P("fsdp"),
    )
    return jax.shard_map(body, mesh=mesh, in_specs=in_specs, out_specs=out_specs, check_vma=False)
```

time: 346 us -> 270 us (0.78); the launches traced: 341 us -> 270 us
  Pallas kernels: 311 us -> 249 us
  local copies, waits for them, and re-layouts: 17.3 us -> 7.23 us
    pallas_call x1, Pallas kernels: 311 us -> 249 us  [body(): pl.pallas_call(functools.partial(kernel, (X, NREP, R, D, FF)), out_shape=...]
    unnamed x35 -> x16, local copies, waits for them, and re-layouts: 12.4 us -> 2.95 us
    transpose x2 -> x0, other arithmetic: 4.14 us -> none  [the longest x1 4.07 us: body(): fin_dn.astype(F32)]
    convert_element_type x1 -> x3, other arithmetic: 2.02 us -> 5.59 us  [the longest x1 2.48 us: body(): fin_dn.astype(F32)]
where the time goes in v2:
time: 270 us
  Pallas kernels  249 us (92%)
  other arithmetic  12.8 us (5%)
  local copies, waits for them, and re-layouts  7.23 us (3%)
    pallas_call x1, Pallas kernels, body(): pl.pallas_call(functools.partial(kernel, (X, NREP, R, D, FF)), out_shape=...  249 us

profile of v2, /device:TPU:0, one launch (start us, length us, event | category | flops | bytes accessed | tf_op | source)
XLA Modules:
  0.0 269.8 jit_solution(6538784892632542720)
XLA Ops:
  0.6 0.8 convert_add_fusion
  1.4 0.6 reshape.63.sm_ref
  2.0 0.7 fusion
  2.7 0.1 reshape.66
  2.8 0.7 broadcast_in_dim.15.oh_ref
  3.5 249.1 %shard_map.263 = (bf16[256,4096]{1,0:T(8,128)(2,1)}, bf16[1024,1024]{1,0:T(8,128)(2,1)}, bf16[256,3072]{1,0:T(8,128)(2,1)}, bf16[256,1024]{1,0:T(8,128)(2,1)}, b...) custom-call(bf16[512,1024]{1,0:T(8,128)(2,1)} %bitcast.16, ...), custom_call_target="tpu_custom_call" | custom-call | tf_op jit(solution)/shard_map/pallas_call | solution.py:945
  252.6 1.5 fusion.1
  254.1 0.0 copy-start.5
  254.1 0.8 dynamic-slice_bitcast_fusion
  254.9 0.6 copy.30
  255.5 0.8 dynamic-slice.4
  256.3 0.6 reshape.64
  256.9 0.0 copy-start
  256.9 4.2 %convert_element_type.51 = f32[256,4096]{1,0:T(8,128)} convert(bf16[256,4096]{1,0:T(8,128)(2,1)} %get-tuple-element.26) | non-fusion elementwise | flops 1048576 | bytes 6291456 | tf_op jit(solution)/shard_map/convert_element_type | solution.py:1009
  261.1 0.0 copy-done
  261.1 0.0 copy-start.1
  261.1 2.5 convert_element_type.52
  263.6 0.0 copy-done.1
  263.6 0.0 copy-start.2
  263.6 2.0 convert_element_type.49
  265.6 0.0 copy-start.4
  265.6 0.0 copy-done.2
  265.6 0.0 copy-start.3
  265.6 1.6 bitcast_convert_fusion
  267.2 0.0 copy-done.4
  267.2 1.1 convert_element_type.50
  268.3 0.0 copy-done.5
  268.3 0.6 copy.33
  268.9 0.0 copy-done.3
  268.9 1.0 copy.34
Async XLA Ops:
  254.1 14.2 %copy-start.5 = (f32[1,256]{1,0:T(1,128)}, f32[1,256]{1,0:T(1,128)S(1)}, u32[]{:S(2)}) copy-start(f32[1,256]{1,0:T(1,128)S(1)} %get-tuple-element.28) | copy-start | bytes 3076
  256.9 4.3 %copy-start = (bf16[1024,1024]{1,0:T(8,128)(2,1)S(1)}, bf16[1024,1024]{1,0:T(8,128)(2,1)}, u32[]{:S(2)}) copy-start(bf16[1024,1024]{1,0:T(8,128)(2,1)} %get-tuple-element.27) | copy-start | bytes 6291460
  261.1 2.5 copy-start.1
  263.6 2.0 copy-start.2
  265.6 1.6 copy-start.4
  265.6 3.2 %copy-start.3 = (bf16[512,1024]{1,0:T(8,128)(2,1)S(1)}, bf16[512,1024]{1,0:T(8,128)(2,1)}, u32[]{:S(2)}) copy-start(bf16[512,1024]{1,0:T(8,128)(2,1)} %get-tuple-element.21) | copy-start | bytes 3145732

commit v3 on v2

--- a/solution.py
+++ b/solution.py
@@ -127,10 +127,12 @@
     finals = []
 
     NG = 4
-    gxs = [S() for _ in range(NG)]
-    gxr = [S() for _ in range(NG)]
-    gzs = [S() for _ in range(NG)]
-    gzr = [S() for _ in range(NG)]
+    units = [(0, 0), (0, 1), (1, 0), (1, 1), (2, 0), (3, 0)]
+    cuts = [2, 2, 1, 1]
+    gxs = [S() for _ in units]
+    gxr = [S() for _ in units]
+    gzs = [S() for _ in units]
+    gzr = [S() for _ in units]
     gcs = [S() for _ in range(NG)]
     gcr = [S() for _ in range(NG)]
     gl = [S() for _ in range(NG)]
@@ -159,7 +161,7 @@
 
     def xz_bytes(k):
         if k < 2:
-            return gbuf.at[pl.ds(0, 2), pl.ds(0, X - 1)]
+            return gbuf.at[0, pl.ds(0, X - 1)]
         return gbuf.at[pl.ds(0, 3 if k == 2 else 1), pl.ds(0, X - 1), pl.ds(0, RX // 2)]
 
     def core_bytes(k):
@@ -175,48 +177,53 @@
     def rows_of(k):
         return (wdn_ref, FX) if k == 1 else (wo_ref, HX)
 
-    def gather_x(k):
+    def gather_x(u):
+        k, cut = units[u]
         for dx in range(1, X):
             xo = lax.rem(xi + dx, X)
             if k in (0, 2):
-                n = RS // 2
-                r0 = mult(q * n, n)
+                n = RS // 2 // cuts[k]
+                r0 = mult(q * (RS // 2) + cut * n, n)
                 for ct in range(2):
                     for src, sc, dc, w in cols(k, ct):
                         rcopy(
                             part(src, r0, n, sc, w),
                             part(dest[k], mult(RS * f + r0, n), n, dc, w),
-                            gxs[k],
-                            gxr[k],
+                            gxs[u],
+                            gxr[u],
                             fsdp=2 * xo + ct,
                         )
             else:
                 src, w = rows_of(k)
-                n = w // 2
+                n = w // 2 // cuts[k]
+                r0 = q * (w // 2) + cut * n
                 rcopy(
-                    span(src, mult(w * y + q * n, n), n),
-                    span(dest[k], mult(w * xi + q * n, n), n),
-                    gxs[k],
-                    gxr[k],
+                    span(src, mult(w * y + r0, n), n),
+                    span(dest[k], mult(w * xi + r0, n), n),
+                    gxs[u],
+                    gxr[u],
                     fsdp=2 * xo + c,
                 )
-        finals.append(lambda: wait(gxs[k], xz_bytes(k)))
-
-    def gather_fwd(k):
-        wait(gxr[k], xz_bytes(k))
+        finals.append(lambda: wait(gxs[u], xz_bytes(k)))
+
+    def gather_fwd(u):
+        k, cut = units[u]
+        wait(gxr[u], xz_bytes(k))
         for dx in range(1, X):
             xo = lax.rem(xi + dx, X)
             if k in (0, 2):
-                n = RS // 2
+                n = RS // 2 // cuts[k]
+                r0 = q * (RS // 2) + cut * n
                 for ct in range(2):
-                    piece = span(dest[k], mult(RS * (2 * xo + ct) + q * n, n), n)
-                    rcopy(piece, piece, gzs[k], gzr[k], rep=zp)
+                    piece = span(dest[k], mult(RS * (2 * xo + ct) + r0, n), n)
+                    rcopy(piece, piece, gzs[u], gzr[u], rep=zp)
             else:
                 _, w = rows_of(k)
-                piece = span(dest[k], mult(w * xo + q * (w // 2), w // 2), w // 2)
-                rcopy(piece, piece, gzs[k], gzr[k], rep=zp)
+                n = w // 2 // cuts[k]
+                piece = span(dest[k], mult(w * xo + q * (w // 2) + cut * n, n), n)
+                rcopy(piece, piece, gzs[u], gzr[u], rep=zp)
         if k > 1:
-            finals.append(lambda: wait(gzs[k], xz_bytes(k)))
+            finals.append(lambda: wait(gzs[u], xz_bytes(k)))
 
     def gather_core(k):
         if k in (0, 2):
@@ -236,7 +243,9 @@
         wait(gl[k], local_bytes(k))
         if k in (0, 2):
             wait(gcr[k], core_bytes(k))
-        wait(gzr[k], xz_bytes(k))
+        for u, (kk, _) in enumerate(units):
+            if kk == k:
+                wait(gzr[u], xz_bytes(k))
 
     xs = [S() for _ in range(NP)]
     xr = [S() for _ in range(NP)]
@@ -249,6 +258,7 @@
     agl = [S() for _ in range(NP)]
     lp = [S() for _ in range(2)]
     held = []
+    made = [0]
 
     h = NREP // 2
     depth = jnp.where(r < h, r, NREP - 1 - r)
@@ -408,13 +418,15 @@
 
     def flush():
         while held:
-            p, gst = held.pop(0)
-            wait(lp[p % 2], gst)
+            p, b, gst = held.pop(0)
+            wait(lp[b], gst)
             ready.append(p)
         push()
 
     def grad_piece(p, lhs_t, rhs, both):
-        gst = both.at[p % 2]
+        made[0] += 1
+        turn = made[0] % 2
+        gst = both.at[turn]
         if is_up(p) or p < 2 * NU:
 
             def step(t, carry):
@@ -431,8 +443,8 @@
                     ]
         own[p] = gst[xi]
         flush()
-        lcopy(gst, gbuf.at[p], lp[p % 2])
-        held.append((p, gst))
+        lcopy(gst, gbuf.at[p], lp[turn])
+        held.append((p, turn, gst))
 
     bar = pltpu.get_barrier_semaphore()
     near = []
@@ -447,6 +459,7 @@
     pl.semaphore_wait(bar, len(near))
 
     gather_x(0)
+    gather_x(1)
     tok = []
     home = ds(2 * c + y, R)
     for src, dst in ((x_ref, X4), (g_ref, G4)):
@@ -520,11 +533,10 @@
             ],
             1,
         )
-        gather_fwd(0)
-        gather_x(1)
-        gather_fwd(1)
-        gather_x(2)
-        gather_x(3)
+        for u in range(4):
+            gather_fwd(u)
+            if u + 2 < len(units):
+                gather_x(u + 2)
         gather_wait(0)
         gather_wait(1)
         half_tiles = T // TT // 2
@@ -569,8 +581,8 @@
                         row = 5 + 2 * yy + rr
                         sgv[row : row + 1, ds(2 * xx + c, RS)] = gb[:, at : at + RS]
 
-        gather_fwd(2)
-        gather_fwd(3)
+        gather_fwd(4)
+        gather_fwd(5)
         for t in range(NU):
             grad_piece(t, n2t, lambda: gup[:, t * PW : (t + 1) * PW], gst)
         for t in range(NU):
@@ -594,21 +606,26 @@
     s_sga, r_sga, l_sga = S(), S(), S()
     s_sgb, r_sgb, l_sgb = S(), S(), S()
 
-    def give(a, buf):
-        rcopy(buf.at[ds(1 - c, L)], mo.at[a], s_mo[a], r_mo[a], fsdp=fs)
-
-    def take(a, buf, room):
-        wait(r_mo[a], mo.at[a])
-        wait(gzs[a], xz_bytes(a))
-        lcopy(mo.at[a], room.at[pl.ds(0, L)], l_st).wait()
-
-        def add(i, carry):
-            rows = pl.ds(mult(c * L + i * 64, 64), 64)
-            buf[rows, :] = (buf[rows, :].astype(F32) + room[ds(i, 64), :].astype(F32)).astype(BF)
-            return carry
-
-        lax.fori_loop(0, L // 64, add, 0)
-        rcopy(buf.at[ds(2 * c + yo, R)], af.at[a], s_af[a], r_af[a], ctx=yo)
+    def give(a, buf, cc):
+        @pl.when(c != cc)
+        def _():
+            rcopy(buf.at[pl.ds(cc * L, L)], mo.at[a], s_mo[a], r_mo[a], fsdp=fs)
+
+    def take(a, buf, room, cc):
+        @pl.when(c == cc)
+        def _():
+            wait(r_mo[a], mo.at[a])
+            lcopy(mo.at[a], room.at[pl.ds(0, L)], l_st).wait()
+
+            def add(i, carry):
+                rows = pl.ds(mult(cc * L + i * 64, 64), 64)
+                buf[rows, :] = (buf[rows, :].astype(F32) + room[ds(i, 64), :].astype(F32)).astype(
+                    BF
+                )
+                return carry
+
+            lax.fori_loop(0, L // 64, add, 0)
+            rcopy(buf.at[ds(2 * cc + yo, R)], af.at[a], s_af[a], r_af[a], ctx=yo)
 
     def last(a, buf, room, dst):
         wait(r_af[a], af.at[a])
@@ -716,84 +733,95 @@
         low_half = lax.broadcasted_iota(jnp.int32, (1, 128), 1) < HEAD
         dkv[...] = jnp.zeros_like(dkv)
         pairs = HC // 128
-        for i in range(NB):
-            n = (i + 1) * TT
-
-            def pair(u, carry):
-                cc, hp = lax.div(u, pairs), lax.rem(u, pairs)
-                lanes = pl.ds(mult(hp * 128, 128), 128)
-                rows = pl.ds(mult(cc * L + i * TT, TT), TT)
-                seen = pl.ds(mult(cc * L, L), n)
-                qb = qkv[0, rows, lanes]
-                gb = gctx[rows, lanes]
-                kb = qkv[1, seen, lanes]
-                vb = qkv[2, seen, lanes]
-                ahead = lax.broadcasted_iota(jnp.int32, (TT, n), 1) - lax.broadcasted_iota(
-                    jnp.int32, (TT, n), 0
-                )
-                zero = jnp.zeros_like(qb)
-                res = []
-                for hd in range(2):
-                    mask = low_half if hd == 0 else jnp.logical_not(low_half)
-                    s = mm(jnp.where(mask, qb, zero), kb, NT)
-                    s = jnp.where(ahead <= i * TT, s, -1e30)
-                    p = jnp.exp(s - jnp.max(s, -1, keepdims=True))
-                    p = p * (1.0 / jnp.sum(p, -1, keepdims=True))
-                    pb = p.astype(BF)
-                    dp = mm(jnp.where(mask, gb, zero), vb, NT)
-                    dsc = (p * (dp - jnp.sum(p * dp, -1, keepdims=True))).astype(BF)
-                    res.append((mm(pb, vb), mm(dsc, kb), mm(dsc, qb, TN), mm(pb, gb, TN)))
-                both = [jnp.where(low_half, u0, u1) for u0, u1 in zip(res[0], res[1])]
-                cb = both[0].astype(BF)
-                ctx[rows, lanes] = cb
-                ctxt[lanes, rows] = cb.T
-                dq = turned(both[1] * (1.0 / math.sqrt(HEAD)), pl.ds(i * TT, TT), -1.0)
-                gproj[rows, lanes] = dq.astype(BF)
-                dkv[0, seen, lanes] += both[2]
-                dkv[1, seen, lanes] += both[3]
+        for u in range(4):
+            wait(gzs[u], xz_bytes(u // 2))
+        for cc in range(2):
+            for i in range(NB):
+                n = (i + 1) * TT
+
+                def pair(hp, carry):
+                    lanes = pl.ds(mult(hp * 128, 128), 128)
+                    rows = pl.ds(cc * L + i * TT, TT)
+                    seen = pl.ds(cc * L, n)
+                    qb = qkv[0, rows, lanes]
+                    gb = gctx[rows, lanes]
+                    kb = qkv[1, seen, lanes]
+                    vb = qkv[2, seen, lanes]
+                    ahead = lax.broadcasted_iota(jnp.int32, (TT, n), 1) - lax.broadcasted_iota(
+                        jnp.int32, (TT, n), 0
+                    )
+                    zero = jnp.zeros_like(qb)
+                    res = []
+                    for hd in range(2):
+                        mask = low_half if hd == 0 else jnp.logical_not(low_half)
+                        s = mm(jnp.where(mask, qb, zero), kb, NT)
+                        s = jnp.where(ahead <= i * TT, s, -1e30)
+                        p = jnp.exp(s - jnp.max(s, -1, keepdims=True))
+                        p = p * (1.0 / jnp.sum(p, -1, keepdims=True))
+                        pb = p.astype(BF)
+                        dp = mm(jnp.where(mask, gb, zero), vb, NT)
+                        dsc = (p * (dp - jnp.sum(p * dp, -1, keepdims=True))).astype(BF)
+                        res.append((mm(pb, vb), mm(dsc, kb), mm(dsc, qb, TN), mm(pb, gb, TN)))
+                    both = [jnp.where(low_half, u0, u1) for u0, u1 in zip(res[0], res[1])]
+                    cb = both[0].astype(BF)
+                    ctx[rows, lanes] = cb
+                    ctxt[lanes, rows] = cb.T
+                    dq = turned(both[1] * (1.0 / math.sqrt(HEAD)), pl.ds(i * TT, TT), -1.0)
+                    gproj[rows, lanes] = dq.astype(BF)
+                    dkv[0, seen, lanes] += both[2]
+                    dkv[1, seen, lanes] += both[3]
+                    return carry
+
+                lax.fori_loop(0, pairs, pair, 0)
+                tick(1)
+                if cc == 1 and i == 1:
+                    take(0, OB, wup, 0)
+                    take(1, TB, wdn, 0)
+
+            if cc == 1:
+                grad_piece(2 * NU, ctxt, lambda: ga[...], gst)
+                grad_piece(2 * NU + 1, n1t, lambda: gproj[:, 0:HC], gst)
+
+            def turn_back(b, carry):
+                t = cc * NB + b
+                for u in range(pairs):
+                    at = pl.ds(u * 128, 128)
+                    gproj[ds(t), HC + u * 128 : HC + (u + 1) * 128] = turned(
+                        dkv[0, ds(t), at], ds(b), -1.0
+                    ).astype(BF)
+                gproj[ds(t), 2 * HC : 3 * HC] = dkv[1, ds(t), :].astype(BF)
                 return carry
 
-            lax.fori_loop(0, 2 * pairs, pair, 0)
-            tick(1)
-
-        def turn_back(t, carry):
-            b = lax.rem(t, NB)
-            for u in range(pairs):
-                at = pl.ds(u * 128, 128)
-                gproj[ds(t), HC + u * 128 : HC + (u + 1) * 128] = turned(
-                    dkv[0, ds(t), at], ds(b), -1.0
-                ).astype(BF)
-            gproj[ds(t), 2 * HC : 3 * HC] = dkv[1, ds(t), :].astype(BF)
-            return carry
-
-        lax.fori_loop(0, T // TT, turn_back, 0)
-
-        grad_piece(2 * NU, ctxt, lambda: ga[...], gst)
-        for m in range(3):
-            grad_piece(2 * NU + 1 + m, n1t, lambda: gproj[:, m * HC : (m + 1) * HC], gst)
-        flush()
-
-        def att_out(t, carry):
-            cc, s = lax.div(t, NB), lax.rem(t, NB)
-            a = mm(in_slot(ctx, cc, s, HC), wo[...])
-            OB[ds(t), :] = (OB[ds(t), :].astype(F32) + a).astype(BF)
-            return carry
-
-        lax.fori_loop(0, T // TT, att_out, 0)
-        give(0, OB)
-        tick(1)
-
-        def att_in(t, carry):
-            cc, s = lax.div(t, NB), lax.rem(t, NB)
-            e = mm(in_slot(gproj, cc, s, 3 * HC), wqkv[...], NT)
-            n, rs = center(X4[ds(t), :])
-            term = norm_back(e, n, rs, vec(0), 0)
-            TB[ds(t), :] = (TB[ds(t), :].astype(F32) + term).astype(BF)
-            return carry
-
-        take(0, OB, wup)
-        lax.fori_loop(0, T // TT, att_in, 0)
-        give(1, TB)
+            lax.fori_loop(0, NB, turn_back, 0)
+            if cc == 1:
+                for m in (2, 1):
+                    grad_piece(2 * NU + 1 + m, n1t, lambda: gproj[:, m * HC : (m + 1) * HC], gst)
+                flush()
+
+            def att_out(s, carry):
+                t = cc * NB + s
+                a = mm(in_slot(ctx, cc, s, HC), wo[...])
+                OB[ds(t), :] = (OB[ds(t), :].astype(F32) + a).astype(BF)
+                return carry
+
+            lax.fori_loop(0, NB, att_out, 0)
+            give(0, OB, cc)
+            if cc == 1:
+                tick(1)
+
+            def att_in(s, carry):
+                t = cc * NB + s
+                e = mm(in_slot(gproj, cc, s, 3 * HC), wqkv[...], NT)
+                n, rs = center(X4[ds(t), :])
+                term = norm_back(e, n, rs, vec(0), 0)
+                TB[ds(t), :] = (TB[ds(t), :].astype(F32) + term).astype(BF)
+                return carry
+
+            lax.fori_loop(0, NB, att_in, 0)
+            give(1, TB, cc)
+            if cc == 1:
+                take(0, OB, wup, 1)
+                tick(1)
 
         for m in range(3):
             gb = jnp.sum(gproj[:, m * HC : (m + 1) * HC].astype(F32), 0, keepdims=True)
@@ -826,7 +854,8 @@
     for dev in near[: 4 * X - 1]:
         rcopy(sgv, sgA.at[here], s_sga, r_sga, **dev)
     tick(1)
-    take(1, TB, wdn)
+    take(1, TB, wdn, 1)
+    tick(1)
     wait(l_sga, sgv)
     wait(r_sga, sgA.at[pl.ds(0, 4 * X - 1)])
     total = sgA[0]
@@ -838,7 +867,6 @@
     for dev in near[4 * X - 1 :]:
         rcopy(sgv, sgB.at[r], s_sgb, r_sgb, **dev)
     tick(1)
-    tick(1, True)
     tick(1, True)
     last(0, OB, wup, out_ref)
     wait(l_sgb, sgv)
@@ -873,7 +901,7 @@
 
 
 def sem_count(NP):
-    return 7 * 4 + 9 * NP + 64
+    return 4 * 6 + 3 * 4 + 9 * NP + 64
 
 
 def body(

time: 270 us -> 264 us (0.978)
  Pallas kernels: 249 us -> 243 us
    pallas_call x1, Pallas kernels: 249 us -> 243 us  [body(): pl.pallas_call(functools.partial(kernel, (X, NREP, R, D, FF)), out_shape=...]
where the time goes in v3:
time: 264 us
  Pallas kernels  243 us (92%)
  other arithmetic  12.8 us (5%)
  local copies, waits for them, and re-layouts  7.23 us (3%)
    pallas_call x1, Pallas kernels, body(): pl.pallas_call(functools.partial(kernel, (X, NREP, R, D, FF)), out_shape=...  243 us

profile of v3, /device:TPU:0, one launch (start us, length us, event | category | flops | bytes accessed | tf_op | source)
XLA Modules:
  0.0 263.7 jit_solution(4136764521581898618)
XLA Ops:
  0.6 0.8 convert_add_fusion
  1.4 0.6 reshape.63.sm_ref
  2.0 0.7 fusion
  2.7 0.1 reshape.66
  2.8 0.7 broadcast_in_dim.15.oh_ref
  3.5 243.0 %shard_map.263 = (bf16[256,4096]{1,0:T(8,128)(2,1)}, bf16[1024,1024]{1,0:T(8,128)(2,1)}, bf16[256,3072]{1,0:T(8,128)(2,1)}, bf16[256,1024]{1,0:T(8,128)(2,1)}, b...) custom-call(bf16[512,1024]{1,0:T(8,128)(2,1)} %bitcast.16, ...), custom_call_target="tpu_custom_call" | custom-call | tf_op jit(solution)/shard_map/pallas_call | solution.py:973
  246.5 1.5 fusion.1
  248.0 0.0 copy-start.5
  248.0 0.8 dynamic-slice_bitcast_fusion
  248.8 0.6 copy.30
  249.4 0.8 dynamic-slice.4
  250.2 0.6 reshape.64
  250.8 0.0 copy-start
  250.8 4.2 %convert_element_type.51 = f32[256,4096]{1,0:T(8,128)} convert(bf16[256,4096]{1,0:T(8,128)(2,1)} %get-tuple-element.26) | non-fusion elementwise | flops 1048576 | bytes 6291456 | tf_op jit(solution)/shard_map/convert_element_type | solution.py:1037
  255.0 0.0 copy-done
  255.0 0.0 copy-start.1
  255.0 2.5 convert_element_type.52
  257.5 0.0 copy-done.1
  257.5 0.0 copy-start.2
  257.5 2.0 convert_element_type.49
  259.5 0.0 copy-start.4
  259.5 0.0 copy-done.2
  259.5 0.0 copy-start.3
  259.5 1.6 bitcast_convert_fusion
  261.1 0.0 copy-done.4
  261.1 1.1 convert_element_type.50
  262.2 0.0 copy-done.5
  262.2 0.6 copy.33
  262.8 0.0 copy-done.3
  262.8 1.0 copy.34
Async XLA Ops:
  248.0 14.2 %copy-start.5 = (f32[1,256]{1,0:T(1,128)}, f32[1,256]{1,0:T(1,128)S(1)}, u32[]{:S(2)}) copy-start(f32[1,256]{1,0:T(1,128)S(1)} %get-tuple-element.28) | copy-start | bytes 3076
  250.8 4.3 %copy-start = (bf16[1024,1024]{1,0:T(8,128)(2,1)S(1)}, bf16[1024,1024]{1,0:T(8,128)(2,1)}, u32[]{:S(2)}) copy-start(bf16[1024,1024]{1,0:T(8,128)(2,1)} %get-tuple-element.27) | copy-start | bytes 6291460
  255.0 2.5 copy-start.1
  257.5 2.0 copy-start.2
  259.5 1.6 copy-start.4
  259.5 3.2 %copy-start.3 = (bf16[512,1024]{1,0:T(8,128)(2,1)S(1)}, bf16[512,1024]{1,0:T(8,128)(2,1)}, u32[]{:S(2)}) copy-start(bf16[512,1024]{1,0:T(8,128)(2,1)} %get-tuple-element.21) | copy-start | bytes 3145732
